TPU v7x, 32 devices: a whole 2x2x4 slice. The times are simulated.
32 devices in a mesh: grp: 2 (over y), br: 8 (over z, x), sub: 2 (over core).
Axes of the slice: x: 2, y: 2, z: 4, core: 2. Of those that a mesh axis runs over, the one named last changes fastest.
Arguments:
- charges: bfloat16 [32, 131072], P(None, ('grp', 'br', 'sub')), parts along dimension 1, may hold values from -6 to 6
- order: int32 [131072], P(('grp', 'br', 'sub')), parts along dimension 0, may hold values from 0 to 8191, as said below
- coords: float32 [3, 131072], P(None, ('grp', 'br', 'sub')), parts along dimension 1, may hold values from 0 to 1
- leaf_basis: bfloat16 [1024, 64, 128], P(('grp', 'br', 'sub')), parts along dimension 0, may hold values from -0.5 to 0.5
- leaf_transfer: bfloat16 [1024, 64, 64], P(('grp', 'br', 'sub')), parts along dimension 0, may hold values from -0.375 to 0.375
- branch_transfer: bfloat16 [16, 64, 64], P(('grp', 'br')), parts along dimension 0, may hold values from -0.75 to 0.75
- upper_transfer: bfloat16 [8, 64, 64], P('grp'), parts along dimension 0, may hold values from -0.75 to 0.75
- top_skeleton: float32 [3, 1792], P(None, 'grp'), parts along dimension 1, may hold values from 0 to 1
- near_src: int32 [1024, 27], P(('grp', 'br', 'sub')), parts along dimension 0, may hold values from 0 to 511, as said below
- near_count: int32 [1024], P(('grp', 'br', 'sub')), parts along dimension 0, may hold values from 14 to 27
- far_src: int32 [1024, 6], P(('grp', 'br', 'sub')), parts along dimension 0, may hold values from 0 to 511, as said below
- far_count: int32 [1024], P(('grp', 'br', 'sub')), parts along dimension 0, may hold values from 1 to 6
- top_src: int32 [28, 6], P('grp'), parts along dimension 0, may hold values from 0 to 7, as said below
- top_count: int32 [28], P('grp'), parts along dimension 0, may hold values from 1 to 6
Outputs:
- potential: float32 [32, 131072], P(None, ('grp', 'br', 'sub')), parts along dimension 1
There are 2 independent parts, one for each index of `grp`. A program takes and returns all parts, laid end to end along the dimension named above; each array names one. Nothing has to cross between parts.
Inputs may be any that keep to these rules, and one draw needn't show every extreme that they name: `order`: within each branch the 8192 entries form a permutation: every input position of the branch (its first device's columns first) appears once. `near_src`: entry 0 of each list is the leaf itself; every source lies within 32 leaves of its target; entries at positions near_count or beyond are to be ignored. `far_src`: every source lies within 32 leaves of its target and differs from it; entries at positions far_count or beyond are to be ignored. `top_src`: rows 0 to 7 belong to the branches, the next 4 rows to the level above, the last 2 rows to the level above that; entries are node numbers within the row's level and never the row's own node; entries at positions top_count or beyond are to be ignored.
All inputs are finite; a program needn't handle non-finite values.
Results may differ from a plain program's by a relative error of at most 0.0047.
Values may be sent and summed in bfloat16 or wider, within the bound.
No kernel may reach another device: no remote copies, remote signals or barrier semaphores. Data moves between devices by JAX's collectives and lax.ppermute only.
A program may use at most 64 MiB of HBM per device.

v0:
```python
import functools

import jax
import jax.numpy as jnp
from jax import lax
from jax.experimental import pallas as pl
from jax.experimental.pallas import tpu as pltpu
from jax.sharding import PartitionSpec as P

scale = 1.7320508075688772 / 0.25
f32 = jnp.float32
bf16 = jnp.bfloat16
HIGHEST = lax.Precision.HIGHEST
NT = (((1,), (1,)), ((), ()))
Q = 4
UNROLL = 3
WIDE = 32
FEAT = 16
CHUNK = 256
VMEM = pl.BlockSpec(memory_space=pltpu.VMEM)
SMEM = pl.BlockSpec(memory_space=pltpu.SMEM)
HBM = pl.BlockSpec(memory_space=pltpu.HBM)
params = pltpu.CompilerParams(vmem_limit_bytes=28 << 20)


def profile_of(squared):
    squared = jnp.maximum(squared, 1e-12)
    scaled = squared * lax.rsqrt(squared)
    return (1.0 + scaled) * jnp.exp(-scaled)


def split(x):
    first = x.astype(bf16).astype(f32)
    rest = x - first
    second = rest.astype(bf16).astype(f32)
    return first, second, (rest - second).astype(bf16).astype(f32)


def permute(rows, order, store, extra, hots, picks, rhs):
    per = CHUNK // order.shape[1]
    groups = rows.shape[0] // rhs
    blocks = order.shape[0] // per
    cuts = 8

    def within(c):
        return jnp.clip(c, 0, blocks - 1)

    def where_from(c):
        return jnp.concatenate([order[pl.ds(within(c) * per + i, 1), :] for i in range(per)], axis=1)

    def step(i, state):
        for u in range(2):
            c = 2 * i + u
            low = where_from(c) & (CHUNK - 1)
            high = where_from(c - 2) >> (CHUNK.bit_length() - 1)
            at = pl.ds(pl.multiple_of(within(c - 2) * CHUNK, CHUNK), CHUNK)
            found = jnp.zeros((rhs, CHUNK), f32)
            tall = rows.shape[0] // cuts
            for k in range(cuts):
                part = slice(k * tall, (k + 1) * tall)
                picks[u][part, :] = jnp.dot(rows[part, :], hots[1 - u][...], preferred_element_type=f32)
                for h in range(k * groups // cuts, (k + 1) * groups // cuts):
                    found = jnp.where(high == h, picks[1 - u][h * rhs : (h + 1) * rhs, :], found)
                lines = CHUNK // cuts
                line = lax.broadcasted_iota(jnp.int32, (lines, CHUNK), 0) + k * lines
                hots[u][k * lines : (k + 1) * lines, :] = jnp.where(line == low, 1.0, 0.0).astype(bf16)
            store(at, found.astype(bf16))
            extra(c, u, within)
        return state

    lax.fori_loop(0, (blocks + 5) // 2, step, 0)


def make_list(flag, source, none, height):
    leaves, near = flag.shape
    flags = jnp.where(flag, 1.0, 0.0)
    before = lax.broadcasted_iota(jnp.int32, (near, near), 0) < lax.broadcasted_iota(jnp.int32, (near, near), 1)
    rank = jnp.dot(flags.astype(bf16), jnp.where(before, 1.0, 0.0).astype(bf16), preferred_element_type=f32)
    number = jnp.sum(flags, axis=1, keepdims=True).astype(jnp.int32)
    even = (number + (number & 1)).astype(f32)
    above = lax.broadcasted_iota(jnp.int32, (leaves, leaves), 1) < lax.broadcasted_iota(jnp.int32, (leaves, leaves), 0)
    start = jnp.dot(
        jnp.where(above, 1.0, 0.0).astype(bf16),
        jnp.broadcast_to(even, (leaves, near)).astype(bf16),
        preferred_element_type=f32,
    )
    place = jnp.where(flag, (start + rank).astype(jnp.int32) + 4 * Q, -1)
    high, low = place >> (WIDE.bit_length() - 1), place & (WIDE - 1)
    lane = lax.broadcasted_iota(jnp.int32, (leaves, 2 * WIDE), 1)
    leaf = lax.broadcasted_iota(jnp.int32, (leaves, 2 * WIDE), 0)
    line = lax.broadcasted_iota(jnp.int32, (leaves, height), 1)
    left, right = [], []
    for j in range(near):
        left.append(jnp.where(line == high[:, j : j + 1], 1.0, 0.0).astype(bf16))
        value = jnp.where(lane < WIDE, leaf, source[:, j : j + 1] + 1)
        right.append(jnp.where((lane & (WIDE - 1)) == low[:, j : j + 1], value, 0).astype(f32).astype(bf16))
    out = lax.dot_general(
        jnp.concatenate(left, axis=0),
        jnp.concatenate(right, axis=0),
        (((0,), (0,)), ((), ())),
        preferred_element_type=f32,
    ).astype(jnp.int32)
    found = out[:, WIDE:]
    code = out[:, :WIDE] * 256 + 2 * jnp.where(found == 0, none, found - 1)
    shape = (height, WIDE)
    last = lax.broadcasted_iota(jnp.int32, shape, 0) * WIDE + lax.broadcasted_iota(jnp.int32, shape, 1)
    pairs = (jnp.sum(even, axis=0, keepdims=True) * 0.5).astype(jnp.int32)
    return jnp.where(last == height * WIDE - 1, pairs, code)


def prepare(*refs):
    fetched = 14
    sources = refs[:fetched]
    charges, order, near_tab, far_tab = refs[fetched : fetched + 4]
    kept = refs[fetched + 4 : fetched + 13]
    feats, tall = refs[fetched + 13 : fetched + 15]
    coords, near_src, near_count, wide, high, sems, coded, code_sems = refs[fetched + 15 :]
    copies = [
        pltpu.make_async_copy(source, dest, sems.at[i])
        for i, (source, dest) in enumerate(
            zip(sources, (charges, order, coords, near_src, near_count) + tuple(kept))
        )
    ]
    for copy in copies:
        copy.start()
    leaves = order.shape[0]
    first = lax.axis_index(("br", "sub")) * leaves
    for i in (3, 4):
        copies[i].wait()
    near = near_src.shape[1]
    square = (leaves, leaves)
    diagonal = lax.broadcasted_iota(jnp.int32, square, 0) == lax.broadcasted_iota(jnp.int32, square, 1)
    live = jnp.sum(jnp.where(diagonal, near_count[...], 0), axis=1, keepdims=True)
    valid = lax.broadcasted_iota(jnp.int32, (leaves, near), 1) < live
    offset = near_src[...] - first
    here = (offset >= 0) & (offset < leaves)
    height = coded.shape[1]
    coded[0] = make_list(here & valid, offset, leaves, height)
    coded[1] = make_list(jnp.logical_not(here) & valid, offset + leaves, 3 * leaves, height)
    code_copies = [
        pltpu.make_async_copy(coded.at[i], dest, code_sems.at[i]) for i, dest in enumerate((near_tab, far_tab))
    ]
    for copy in code_copies:
        copy.start()
    wide[...] = jnp.zeros_like(wide)
    high[...] = jnp.zeros_like(high)
    copies[2].wait()
    place = (coords[...] - 0.5) * scale
    r1, r2, r3 = split(place)
    n1, n2, n3 = split(
        place[0:1] * place[0:1] + place[1:2] * place[1:2] + place[2:3] * place[2:3]
    )
    one = jnp.ones_like(n1)
    wide[0:3, :] = -2.0 * r1
    wide[3:6, :] = -2.0 * r2
    wide[6:9, :] = -2.0 * r3
    wide[9:10, :] = n1
    wide[10:11, :] = n2
    wide[11:12, :] = n3
    wide[12:13, :] = one
    feats[...] = wide[...].astype(bf16)
    for i in range(3):
        high[3 * i : 3 * i + 3, :] = r1
        high[9 + i : 10 + i, :] = one
    high[12:13, :] = n1
    high[16:19, :] = r2
    high[19:22, :] = r2
    high[28:29, :] = n2
    high[32:35, :] = r3
    high[44:45, :] = n3
    tall[...] = high[...].astype(bf16)
    for copy in code_copies:
        copy.wait()
    for i in (0, 1, *range(5, fetched)):
        copies[i].wait()


def turn(tall, target):
    width = tall.shape[1]
    square = (128, 128)
    one = jnp.where(
        lax.broadcasted_iota(jnp.int32, square, 0) == lax.broadcasted_iota(jnp.int32, square, 1), 1.0, 0.0
    ).astype(bf16)
    for at in range(0, width, 128):
        target[at : at + 128, :] = lax.dot_general(
            one, tall[:, at : at + 128], NT, preferred_element_type=f32
        ).astype(bf16)


def table_height(leaves, near):
    need = 4 * Q + leaves * (near + near % 2) + 2 * Q * (UNROLL + 4) + 1
    return -(-need // (8 * WIDE)) * 8


def upward(
    charges, partner, order, feats, basis, transfer, branch_transfer, upper_transfer,
    pack, up, rows, packed, *pipes,
):
    leaves, points = order.shape
    rhs = charges.shape[0]
    rank = basis.shape[1]
    blocks = charges.shape[1] // CHUNK
    own = lax.axis_index("sub") * blocks
    for h in range(blocks):
        for at, ref in ((own + h, charges), (blocks - own + h, partner)):
            rows[pl.ds(pl.multiple_of(at * rhs, rhs), rhs), :] = ref[:, h * CHUNK : (h + 1) * CHUNK]
    pack[rhs : rhs + FEAT, :] = feats[...]
    per = CHUNK // points
    early = lax.broadcasted_iota(jnp.int32, (rhs, 2 * rank), 1) < rank
    hots, picks, raw = pipes[:2], pipes[2:4], pipes[4:]

    def columns(leaf):
        return pl.ds(pl.multiple_of(leaf * points, points), points)

    def extra(c, u, within):
        for pair in range(per // 2):
            lines = slice(2 * rhs * pair, 2 * rhs * (pair + 1))
            leaf = within(c - 4) * per + 2 * pair
            both = raw[1 - u][lines, :]
            coef = jnp.where(early, both[:rhs], both[rhs:])
            turned = pltpu.roll(coef, rank, 1)
            packed[:, columns(leaf >> 1)] = coef.astype(bf16)
            pack[rhs + FEAT :, columns(leaf)] = jnp.where(early, coef, turned).astype(bf16)
            pack[rhs + FEAT :, columns(leaf + 1)] = jnp.where(early, turned, coef).astype(bf16)
            leaf = within(c - 3) * per + 2 * pair
            raw[u][lines, :] = lax.dot_general(
                jnp.concatenate([pack[0:rhs, columns(leaf)], pack[0:rhs, columns(leaf + 1)]], axis=0),
                basis[pl.ds(leaf, 2)].reshape(2 * rank, points),
                NT,
                preferred_element_type=f32,
            )

    def store(at, found):
        pack[0:rhs, at] = found

    permute(rows, order, store, extra, hots, picks, rhs)
    half = rhs // 2
    total = jnp.dot(packed[...], transfer[...].reshape(leaves * rank, rank), preferred_element_type=f32)
    lifted = jnp.dot(total, branch_transfer[0].astype(f32), precision=HIGHEST)
    parent = lax.axis_index("br") // 2
    second = jnp.dot(lifted, upper_transfer[parent].astype(f32), precision=HIGHEST)
    up[0:rhs, 0:rank] = total
    up[0:rhs, rank : 2 * rank] = lifted
    up[rhs : rhs + half, 0:rank] = second[:half]
    up[rhs : rhs + half, rank : 2 * rank] = second[half:]


def near_items(tab, target, sources, values, out, distances, kernels, points):
    total = (tab[tab.shape[0] - 1, WIDE - 1] + Q - 1) // Q
    for distance, kernel in zip(distances, kernels):
        distance[...] = jnp.full(distance.shape, 1e6, f32)
        kernel[...] = jnp.zeros_like(kernel)

    def columns(leaf):
        return pl.ds(pl.multiple_of(leaf * points, points), points)

    def decode(item, q):
        at = (item * Q + q) * 2
        high, low = at >> (WIDE.bit_length() - 1), at & (WIDE - 1)
        one, two = tab[high, low], tab[high, low + 1]
        return columns(one >> 8), columns((one >> 1) & 127), columns((two >> 1) & 127)

    def step(i, _):
        for u in range(UNROLL):
            item = i * UNROLL + u
            behind, last = (u - 1) % UNROLL, (u - 2) % UNROLL
            for q in range(Q):
                part = slice(2 * q * points, 2 * (q + 1) * points)
                leaf, one, two = decode(item, q)
                value = lax.dot_general(
                    jnp.concatenate([values[:, one], values[:, two]], axis=1),
                    kernels[last][:, part],
                    NT,
                    preferred_element_type=f32,
                )
                kernels[behind][:, part] = profile_of(distances[behind][:, part]).astype(bf16)
                target_leaf, one, two = decode(item + 2, q)
                pair = jnp.concatenate([sources[:, one], sources[:, two]], axis=1)
                distances[u][:, part] = jnp.dot(
                    target[target_leaf, :],
                    jnp.concatenate([pair, pair, pair], axis=0),
                    preferred_element_type=f32,
                )
                out[:, leaf] += value
        return 0

    lax.fori_loop(0, (total + 2 + UNROLL - 1) // UNROLL, step, 0)


def near_local(tab, pack, target, out, sources, values, *scratch):
    rhs, width = out.shape
    points = sources.shape[1] - width
    sources[:, :width] = pack[rhs : rhs + FEAT, :]
    sources[:, width:] = jnp.zeros_like(sources[:, width:])
    values[:, :width] = pack[0:rhs, :]
    values[:, width:] = jnp.zeros_like(values[:, width:])
    out[...] = jnp.zeros_like(out)
    near_items(
        tab, target, sources, values, out, scratch[:UNROLL], scratch[UNROLL:], points
    )


def near_remote(
    tab, far_src, far_count, outer, inner, pack, target, start, out, field,
    sources, values, coefs, *scratch
):
    rhs, width = out.shape
    far, leaves = far_src.shape
    points = width // leaves
    rank = field.shape[1] // leaves
    none = 3 * leaves
    side = 2 * lax.axis_index("sub")
    for at, ref in ((side * width, outer), ((2 - side) * width, inner), (width, pack)):
        to = pl.ds(pl.multiple_of(at, width), width)
        sources[:, to] = ref[rhs : rhs + FEAT, :]
        values[:, to] = ref[0:rhs, :]
        coefs[:, to] = ref[rhs + FEAT :, :]
    for ref in (sources, values, coefs):
        ref[:, none * points :] = jnp.zeros_like(ref[:, none * points :])
    out[...] = start[...]
    distances, kernels = scratch[:UNROLL], scratch[UNROLL:]
    near_items(tab, target, sources, values, out, distances, kernels, points)
    early = lax.broadcasted_iota(jnp.int32, (FEAT, points), 1) < rank
    early_values = lax.broadcasted_iota(jnp.int32, (rhs, points), 1) < rank
    base = (lax.axis_index(("br", "sub")) - 1) * leaves

    def columns(leaf):
        return pl.ds(pl.multiple_of(leaf * points, points), points)

    def picked(leaf, j):
        if j >= far:
            return columns(none)
        return columns(jnp.where(j < far_count[leaf], far_src[j, leaf] - base, none))

    items = leaves // 2

    def far_step(i, _):
        for u in range(UNROLL):
            item = i * UNROLL + u
            behind, last = (u - 1) % UNROLL, (u - 2) % UNROLL
            done = jnp.maximum(item - 2, 0)
            ahead = jnp.minimum(item, items - 1)
            total = jnp.zeros((2 * rhs, points), f32)
            for g in range((far + 1) // 2):
                part = slice(g * points, (g + 1) * points)
                pair = []
                for leaf in (2 * done, 2 * done + 1):
                    one, two = picked(leaf, 2 * g), picked(leaf, 2 * g + 1)
                    pair.append(jnp.where(early_values, coefs[:, one], coefs[:, two]))
                total += lax.dot_general(
                    jnp.concatenate(pair, axis=0), kernels[last][:, part], NT, preferred_element_type=f32
                )
                kernels[behind][:, part] = profile_of(distances[behind][:, part]).astype(bf16)
                for k in range(2):
                    leaf = 2 * ahead + k
                    one, two = picked(leaf, 2 * g), picked(leaf, 2 * g + 1)
                    turned = pltpu.roll(sources[:, two].astype(f32), rank, 1)
                    both = jnp.where(early, sources[:, one].astype(f32), turned).astype(bf16)
                    distances[u][k * rank : (k + 1) * rank, part] = jnp.dot(
                        target[pl.ds(pl.multiple_of(leaf * points, points), rank), :],
                        jnp.concatenate([both, both, both], axis=0),
                        preferred_element_type=f32,
                    )
            field[:, columns(done)] = jnp.where(early_values, total[:rhs], total[rhs:])
        return 0

    lax.fori_loop(0, (items + 2 + UNROLL - 1) // UNROLL, far_step, 0)


def downward(
    top_src, top_count, mine, theirs, skeleton, near, field, basis, transfer, branch_transfer, upper_transfer, out, places, every
):
    rhs = near.shape[0]
    leaves, rank, points = basis.shape
    branches = lax.axis_size("br")
    branch = lax.axis_index("br")
    depth = every.shape[0] // branches
    half = rhs // 2
    fan = top_src.shape[0]
    every[0 : mine.shape[0], :] = mine[...]
    every[mine.shape[0] :, :] = theirs[...]
    places[...] = jnp.zeros_like(places)

    def node_places(node):
        both = skeleton[:, pl.ds(pl.multiple_of((node >> 1) * (2 * rank), 2 * rank), 2 * rank)]
        return jnp.where((node & 1) == 1, both[:, rank:], both[:, :rank])

    def coefficients(level, node):
        total = None
        for d in range(1 << level):
            at = pl.multiple_of((((node << level) + d) ^ branch) * depth, 8)
            if level < 2:
                block = every[pl.ds(at, rhs), :]
            else:
                block = every[pl.ds(at + rhs, half), :]
            total = block if total is None else total + block
        if level == 0:
            return total[:, :rank]
        if level == 1:
            return total[:, rank:]
        return jnp.concatenate([total[:, :rank], total[:, rank:]], axis=0)

    offset = 0
    fields = []
    for level in range(3):
        node = branch >> level
        row = offset + node
        places[0:3, 0:rank] = node_places(row)
        own = places[...].T
        kernels, coefs = [], []
        for j in range(fan):
            source = top_src[j, row]
            there = node_places(offset + source)
            squared = None
            for d in range(3):
                gap = (there[d : d + 1, :] - own[0:rank, d : d + 1]) * scale
                squared = gap * gap if squared is None else squared + gap * gap
            kernels.append(profile_of(squared))
            coefs.append(jnp.where(j < top_count[row], coefficients(level, source), 0.0))
        fields.append(
            lax.dot_general(
                jnp.concatenate(coefs, axis=1),
                jnp.concatenate(kernels, axis=1),
                NT,
                precision=HIGHEST,
                preferred_element_type=f32,
            )
        )
        offset += branches >> level
    down_one = fields[1] + lax.dot_general(
        fields[2], upper_transfer[branch >> 1].astype(f32), NT, precision=HIGHEST, preferred_element_type=f32
    )
    down_zero = fields[0] + lax.dot_general(
        down_one, branch_transfer[0].astype(f32), NT, precision=HIGHEST, preferred_element_type=f32
    )
    down_zero = down_zero.astype(bf16)
    lane = lax.broadcasted_iota(jnp.int32, (rhs, 2 * rank), 1)
    for i in range(leaves // 2):
        at = 2 * i * rank
        down = field[:, at : at + 2 * rank] + lax.dot_general(
            down_zero,
            transfer[2 * i : 2 * i + 2].reshape(2 * rank, rank),
            NT,
            preferred_element_type=f32,
        )
        both = jnp.concatenate(
            [jnp.where(lane < rank, down, 0.0), jnp.where(lane < rank, 0.0, down)], axis=0
        ).astype(bf16)
        value = jnp.dot(both, basis[2 * i : 2 * i + 2].reshape(2 * rank, points), preferred_element_type=f32)
        for k in range(2):
            col = (2 * i + k) * points
            out[:, col : col + points] = near[:, col : col + points] + value[k * rhs : (k + 1) * rhs]


def shards(
    charges,
    order,
    coords,
    leaf_basis,
    leaf_transfer,
    branch_transfer,
    upper_transfer,
    top_skeleton,
    near_src,
    near_count,
    far_src,
    far_count,
    top_src,
    top_count,
):
    rhs, width = charges.shape
    leaves, rank, points = leaf_basis.shape
    near = near_src.shape[1]
    branches = lax.axis_size("br")
    height = table_height(leaves, near)
    shape = jax.ShapeDtypeStruct
    like = lambda x: shape(x.shape, x.dtype)
    cost = lambda us: pl.CostEstimate(
        flops=int(us * 1e6), bytes_accessed=int(us * 3e6), transcendentals=0
    )
    swap = [(0, 1), (1, 0)]
    order = order.reshape(leaves, points)
    partner = lax.ppermute(charges, "sub", swap)
    fetched = [
        charges, order, coords, near_src, near_count.reshape(1, leaves),
        leaf_basis, leaf_transfer, branch_transfer, upper_transfer, top_skeleton,
        far_src.T, far_count, top_src.T, top_count,
    ]
    (
        own, order, near_tab, far_tab,
        leaf_basis, leaf_transfer, branch_transfer, upper_transfer, top_skeleton,
        far_src, far_count, top_src, top_count,
        feats, tall,
    ) = pl.pallas_call(
        prepare,
        out_shape=(like(charges), like(order), shape((height, WIDE), jnp.int32), shape((height, WIDE), jnp.int32))
        + tuple(like(x) for x in fetched[5:])
        + (shape((FEAT, width), bf16), shape((3 * FEAT, width), bf16)),
        in_specs=[HBM] * len(fetched),
        out_specs=(VMEM, VMEM, SMEM, SMEM) + (VMEM,) * 5 + (SMEM,) * 4 + (VMEM, VMEM),
        scratch_shapes=[
            pltpu.VMEM(coords.shape, f32),
            pltpu.VMEM(near_src.shape, jnp.int32),
            pltpu.VMEM((1, leaves), jnp.int32),
            pltpu.VMEM((FEAT, width), f32),
            pltpu.VMEM((3 * FEAT, width), f32),
            pltpu.SemaphoreType.DMA((len(fetched),)),
            pltpu.VMEM((2, height, WIDE), jnp.int32),
            pltpu.SemaphoreType.DMA((2,)),
        ],
        compiler_params=params,
        cost_estimate=cost(2),
        name="prepare",
    )(*(pltpu.with_memory_space_constraint(x, pltpu.HBM) for x in fetched))
    chunks = 2 * rhs * width // CHUNK
    pack, up = pl.pallas_call(
        upward,
        out_shape=(
            shape((2 * rhs + FEAT, width), bf16),
            shape((rhs + rhs // 2, 2 * rank), f32),
        ),
        in_specs=[VMEM] * 8,
        out_specs=(VMEM, VMEM),
        scratch_shapes=[
            pltpu.VMEM((chunks, CHUNK), bf16),
            pltpu.VMEM((rhs, leaves * rank), bf16),
            *[pltpu.VMEM((CHUNK, CHUNK), bf16)] * 2,
            *[pltpu.VMEM((chunks, CHUNK), f32)] * 2,
            *[pltpu.VMEM((rhs * CHUNK // points, 2 * rank), f32)] * 2,
        ],
        compiler_params=params,
        cost_estimate=cost(6),
        name="upward",
    )(
        own, partner, order, feats,
        leaf_basis, leaf_transfer, branch_transfer, upper_transfer,
    )
    target = pl.pallas_call(
        turn,
        out_shape=shape((width, 3 * FEAT), bf16),
        in_specs=[VMEM],
        out_specs=VMEM,
        compiler_params=params,
        cost_estimate=cost(1),
        name="turn",
    )(tall)
    up = up + lax.ppermute(up, "sub", swap)
    between = [(2 * j + 1, 2 * j + 2) for j in range(branches - 1)]
    up, held = lax.optimization_barrier((up, pack))
    exchange = lambda x, bit: lax.ppermute(x, "br", [(i, i ^ (1 << bit)) for i in range(branches)])
    theirs, held = lax.optimization_barrier((exchange(up, 0), held))
    outer = lax.ppermute(held, ("br", "sub"), between + [(b, a) for a, b in between])
    inner = lax.ppermute(held, "sub", swap)
    pipeline = [pltpu.VMEM((points, 2 * Q * points), f32)] * UNROLL + [
        pltpu.VMEM((points, 2 * Q * points), bf16)
    ] * UNROLL

    def local():
        return pl.pallas_call(
            near_local,
            out_shape=shape((rhs, width), f32),
            in_specs=[SMEM, VMEM, VMEM],
            out_specs=VMEM,
            scratch_shapes=[
                pltpu.VMEM((FEAT, width + points), bf16),
                pltpu.VMEM((rhs, width + points), bf16),
            ]
            + pipeline,
            compiler_params=params,
            cost_estimate=cost(11),
            name="near_local",
        )(near_tab, held, target)

    mine = up
    for bit in range(1, branches.bit_length() - 1):
        mine = jnp.concatenate([mine, theirs], axis=0)
        theirs = exchange(mine, bit)
        if bit == branches.bit_length() - 3:
            theirs, start = lax.optimization_barrier((theirs, local()))
    both, field = pl.pallas_call(
        near_remote,
        out_shape=(shape((rhs, width), f32), shape((rhs, leaves * rank), f32)),
        in_specs=[SMEM] * 3 + [VMEM] * 5,
        out_specs=(VMEM, VMEM),
        scratch_shapes=[
            pltpu.VMEM((FEAT, 3 * width + points), bf16),
            pltpu.VMEM((rhs, 3 * width + points), bf16),
            pltpu.VMEM((rhs, 3 * width + points), bf16),
        ]
        + pipeline,
        compiler_params=params,
        cost_estimate=cost(14),
        name="near_remote",
    )(far_tab, far_src, far_count, outer, inner, pack, target, start)
    return pl.pallas_call(
        downward,
        out_shape=shape((rhs, width), f32),
        in_specs=[SMEM, SMEM] + [VMEM] * 9,
        out_specs=VMEM,
        scratch_shapes=[
            pltpu.VMEM((8, 128), f32),
            pltpu.VMEM((branches * up.shape[0], 2 * rank), f32),
        ],
        compiler_params=params,
        cost_estimate=cost(4),
        name="downward",
    )(
        top_src, top_count, mine, theirs, top_skeleton, both, field,
        leaf_basis, leaf_transfer, branch_transfer, upper_transfer,
    )


def solution(mesh):
    return jax.shard_map(
        shards,
        mesh=mesh,
        in_specs=(
            P(None, ("grp", "br", "sub")),
            P(("grp", "br", "sub")),
            P(None, ("grp", "br", "sub")),
            P(("grp", "br", "sub"), None, None),
            P(("grp", "br", "sub"), None, None),
            P(("grp", "br"), None, None),
            P("grp", None, None),
            P(None, "grp"),
            P(("grp", "br", "sub"), None),
            P(("grp", "br", "sub")),
            P(("grp", "br", "sub"), None),
            P(("grp", "br", "sub")),
            P("grp", None),
            P("grp"),
        ),
        out_specs=P(None, ("grp", "br", "sub")),
        check_vma=False,
    )
```

profile of v0, /device:TPU:1, one launch (start us, length us, event | category | flops | bytes accessed | tf_op | source)
XLA Modules:
  0.0 56.6 jit_solution(5364173223426708165)
XLA Ops:
  0.0 0.1 collective-permute-start
  0.1 5.2 %prepare.1 = (bf16[32,4096]{1,0:T(8,128)(2,1)S(1)}, s32[32,128]{1,0:T(8,128)S(1)}, s32[32,32]{1,0:T(8,128)S(1)}, s32[32,32]{1,0:T(8,128)S(1)}, bf16[32,64,128]{2...) custom-call(bf16[32,4096]{1,0:T(8,128)(2,1)} %refs_0_.1, ...), custom_call_target="tpu_custom_call" | custom-call | flops 2000000 | bytes 6000000 | tf_op jit(solution)/shard_map/prepare/pallas_call | solution.py:494
  5.3 0.0 collective-permute-done.partner
  5.3 6.4 %upward.1 = (bf16[80,4096]{1,0:T(8,128)(2,1)S(1)}, f32[48,128]{1,0:T(8,128)S(1)}) custom-call(bf16[32,4096]{1,0:T(8,128)(2,1)S(1)} %get-tuple-element.32.charges, bf16[32,4096]{1,0:T(8,128)(2,1)S(1)} %collective-permute-done.partner, s32[32,128]{1,0:T(8,128)S(1)} %get-tuple-element.33.order, bf16[16,4096]{1,0:T(8,128)(2,1)S(1)} %get-tuple-element.34.feats, ...), custom_call_target="tpu_custom_call" | custom-call | flops 6000000 | bytes 18000000 | tf_op jit(solution)/shard_map/upward/pallas_call | solution.py:516
  11.7 0.5 collective-permute-start.1
  12.2 0.8 %collective-permute-done.1 = f32[48,128]{1,0:T(8,128)S(1)} collective-permute-done((f32[48,128]{1,0:T(8,128)S(1)}, f32[48,128]{1,0:T(8,128)S(1)}, u32[]{:S(2)}, u32[]{:S(2)}) %collective-permute-start.1) | collective-permute-done | bytes 24608 | tf_op jit(solution)/shard_map/ppermute | solution.py:547
  13.0 2.5 %collective-permute-start.2 = (f32[48,128]{1,0:T(8,128)S(1)}, f32[48,128]{1,0:T(8,128)S(1)}, u32[]{:S(2)}, u32[]{:S(2)}) collective-permute-start(f32[48,128]{1,0:T(8,128)S(1)} %add.3), channel_id=1, source_target_pairs={{0,2},{2,0},{4,6},{6,4},{8,10},{10,8},{12,14},{14,12},{1,3},{3,1},... | collective-permute-start | bytes 73736 | tf_op jit(solution)/shard_map/ppermute | solution.py:550
  15.6 1.2 %collective-permute-done.2 = f32[48,128]{1,0:T(8,128)S(1)} collective-permute-done((f32[48,128]{1,0:T(8,128)S(1)}, f32[48,128]{1,0:T(8,128)S(1)}, u32[]{:S(2)}, u32[]{:S(2)}) %collective-permute-start.2) | collective-permute-done | bytes 24608 | tf_op jit(solution)/shard_map/ppermute | solution.py:550
  16.8 4.6 %collective-permute-start.5 = (bf16[80,4096]{1,0:T(8,128)(2,1)S(1)}, bf16[80,4096]{1,0:T(8,128)(2,1)S(1)}, u32[]{:S(2)}, u32[]{:S(2)}) collective-permute-start(bf16[80,4096]{1,0:T(8,128)(2,1)S(1)} %get-tuple-element.45.pack), channel_id=1, source_target_pairs={{1,2},{3,4},{5,6},{7,8},{9,10},{11,12},{13,14},{2,1},{4,3},{6,5},{... | collective-permute-start | bytes 1966088 | tf_op jit(solution)/shard_map/ppermute | solution.py:552
  21.4 0.1 collective-permute-start.6
  21.5 0.4 turn.1.target
  21.9 1.4 %collective-permute-start.3 = (f32[96,128]{1,0:T(8,128)S(1)}, f32[96,128]{1,0:T(8,128)S(1)}, u32[]{:S(2)}, u32[]{:S(2)}) collective-permute-start(f32[96,128]{1,0:T(8,128)S(1)} %pad_maximum_fusion), channel_id=1, source_target_pairs={{0,4},{2,6},{4,0},{6,2},{8,12},{10,14},{12,8},{14,10},{1,5},{3,7},... | collective-permute-start | bytes 147464 | tf_op jit(solution)/shard_map/ppermute | solution.py:550
  23.3 10.8 %near_local.1.start = f32[32,4096]{1,0:T(8,128)S(1)} custom-call(s32[32,32]{1,0:T(8,128)S(1)} %get-tuple-element.44.tab, bf16[80,4096]{1,0:T(8,128)(2,1)S(1)} %get-tuple-element.45.pack, bf16[4096,48]{1,0:T(8,128)(2,1)S(1)} %turn.1.target), custom_call_target="tpu_custom_call" | custom-call | flops 11000000 | bytes 33000000 | tf_op jit(solution)/shard_map/near_local/pallas_call | solution.py:559
  34.0 0.0 collective-permute-done.3
  34.0 2.4 %collective-permute-start.4 = (f32[192,128]{1,0:T(8,128)S(1)}, f32[192,128]{1,0:T(8,128)S(1)}, u32[]{:S(2)}, u32[]{:S(2)}) collective-permute-start(f32[192,128]{1,0:T(8,128)S(1)} %constant_dynamic-update-slice_fusion.mine), channel_id=1, source_target_pairs={{0,8},{2,10},{4,12},{6,14},{8,0},{10,2},{12,4},{14,6},{1,9},{3,11}... | collective-permute-start | bytes 294920 | tf_op jit(solution)/shard_map/ppermute | solution.py:550
  36.4 0.0 collective-permute-done.5.outer
  36.4 0.0 collective-permute-done.6.inner
  36.4 14.9 %near_remote.1 = (f32[32,4096]{1,0:T(8,128)S(1)}, f32[32,2048]{1,0:T(8,128)S(1)}) custom-call(s32[32,32]{1,0:T(8,128)S(1)} %get-tuple-element.49.tab, s32[6,32]{1,0:T(8,128)S(1)} %get-tuple-element.50.far_src, s32[32]{0:T(128)S(1)} %get-tuple-element.51.far_count, bf16[80,4096]{1,0:T(8,128)(2,1)S(1)} %collective-permute-done.5.outer, ...), custom_call_target="tpu_custom_call" | custom-call | flops 14000000 | bytes 42000000 | tf_op jit(solution)/shard_map/near_remote/pallas_call | solution.py:580
  51.4 0.0 collective-permute-done.4.theirs
  51.4 5.3 %downward.1 = f32[32,4096]{1,0:T(8,128)} custom-call(s32[6,14]{1,0:T(8,128)S(1)} %get-tuple-element.30.top_src, s32[14]{0:T(128)S(1)} %get-tuple-element.31.top_count, f32[192,128]{1,0:T(8,128)S(1)} %constant_dynamic-update-slice_fusion.mine, f32[192,128]{1,0:T(8,128)S(1)} %collective-permute-done.4.theirs, f32[3,896]{1,0:T(4,128)S(1)} %get-tuple-element.48.skeleton, ...), custom_call_target="tpu_custom_call" | custom-call | flops 4000000 | bytes 12000000 | tf_op jit(solution)/shard_map/downward/pallas_call | solution.py:595
  (5 shorter events, 0.0 us)
Async XLA Ops:
  0.0 5.3 %collective-permute-start = (bf16[32,4096]{1,0:T(8,128)(2,1)}, bf16[32,4096]{1,0:T(8,128)(2,1)S(1)}, u32[]{:S(2)}, u32[]{:S(2)}) collective-permute-start(bf16[32,4096]{1,0:T(8,128)(2,1)} %refs_0_.1), channel_id=1, source_target_pairs={{0,1},{1,0},{2,3},{3,2},{4,5},{5,4},{6,7},{7,6},{8,9},{9,8},{10,11... | collective-permute-start | bytes 786440 | tf_op jit(solution)/shard_map/ppermute | solution.py:483
  11.7 1.3 %collective-permute-start.1 = (f32[48,128]{1,0:T(8,128)S(1)}, f32[48,128]{1,0:T(8,128)S(1)}, u32[]{:S(2)}, u32[]{:S(2)}) collective-permute-start(f32[48,128]{1,0:T(8,128)S(1)} %get-tuple-element.39), channel_id=1, source_target_pairs={{0,1},{1,0},{2,3},{3,2},{4,5},{5,4},{6,7},{7,6},{8,9},{9,8},{10,11... | collective-permute-start | bytes 73736 | tf_op jit(solution)/shard_map/ppermute | solution.py:547
  13.0 3.8 %collective-permute-start.2 = (f32[48,128]{1,0:T(8,128)S(1)}, f32[48,128]{1,0:T(8,128)S(1)}, u32[]{:S(2)}, u32[]{:S(2)}) collective-permute-start(f32[48,128]{1,0:T(8,128)S(1)} %add.3), channel_id=1, source_target_pairs={{0,2},{2,0},{4,6},{6,4},{8,10},{10,8},{12,14},{14,12},{1,3},{3,1},... | collective-permute-start | bytes 73736 | tf_op jit(solution)/shard_map/ppermute | solution.py:550
  16.8 19.6 %collective-permute-start.5 = (bf16[80,4096]{1,0:T(8,128)(2,1)S(1)}, bf16[80,4096]{1,0:T(8,128)(2,1)S(1)}, u32[]{:S(2)}, u32[]{:S(2)}) collective-permute-start(bf16[80,4096]{1,0:T(8,128)(2,1)S(1)} %get-tuple-element.45.pack), channel_id=1, source_target_pairs={{1,2},{3,4},{5,6},{7,8},{9,10},{11,12},{13,14},{2,1},{4,3},{6,5},{... | collective-permute-start | bytes 1966088 | tf_op jit(solution)/shard_map/ppermute | solution.py:552
  21.4 15.0 %collective-permute-start.6 = (bf16[80,4096]{1,0:T(8,128)(2,1)S(1)}, bf16[80,4096]{1,0:T(8,128)(2,1)S(1)}, u32[]{:S(2)}, u32[]{:S(2)}) collective-permute-start(bf16[80,4096]{1,0:T(8,128)(2,1)S(1)} %get-tuple-element.45.pack), channel_id=1, source_target_pairs={{0,1},{1,0},{2,3},{3,2},{4,5},{5,4},{6,7},{7,6},{8,9},{9,8},{10,11... | collective-permute-start | bytes 1966088 | tf_op jit(solution)/shard_map/ppermute | solution.py:553
  21.9 12.1 %collective-permute-start.3 = (f32[96,128]{1,0:T(8,128)S(1)}, f32[96,128]{1,0:T(8,128)S(1)}, u32[]{:S(2)}, u32[]{:S(2)}) collective-permute-start(f32[96,128]{1,0:T(8,128)S(1)} %pad_maximum_fusion), channel_id=1, source_target_pairs={{0,4},{2,6},{4,0},{6,2},{8,12},{10,14},{12,8},{14,10},{1,5},{3,7},... | collective-permute-start | bytes 147464 | tf_op jit(solution)/shard_map/ppermute | solution.py:550
  34.0 17.3 %collective-permute-start.4 = (f32[192,128]{1,0:T(8,128)S(1)}, f32[192,128]{1,0:T(8,128)S(1)}, u32[]{:S(2)}, u32[]{:S(2)}) collective-permute-start(f32[192,128]{1,0:T(8,128)S(1)} %constant_dynamic-update-slice_fusion.mine), channel_id=1, source_target_pairs={{0,8},{2,10},{4,12},{6,14},{8,0},{10,2},{12,4},{14,6},{1,9},{3,11}... | collective-permute-start | bytes 294920 | tf_op jit(solution)/shard_map/ppermute | solution.py:550
where the time goes:
time: 56.5 us; the launch traced here: 56.6 us
  Pallas kernels  43 us (76%)
  starting transfers between devices  11.4 us (20%)
  waiting for transfers between devices  2.08 us (4%)
    pallas_call x1, Pallas kernels, shards(): pl.pallas_call(near_remote, out_shape=(shape((rhs, width), f32), shape((r...  14.9 us
    pallas_call x1, Pallas kernels, local(): pl.pallas_call(near_local, out_shape=shape((rhs, width), f32), in_specs=[...  10.8 us
    pallas_call x1, Pallas kernels, shards(): pl.pallas_call(upward, out_shape=(shape((2 * rhs + FEAT, width), bf16), s...  6.45 us
    ppermute x3, starting transfers between devices, shards(): lax.ppermute(x, 'br', [(i, i ^ 1 << bit) for i in range(branches)])  6.29 us
    pallas_call x1, Pallas kernels, shards(): pl.pallas_call(downward, out_shape=shape((rhs, width), f32), in_specs=[SM...  5.25 us
    pallas_call x1, Pallas kernels, shards(): pl.pallas_call(prepare, out_shape=(like(charges), like(order), shape((hei...  5.2 us
    ppermute x1, starting transfers between devices, shards(): lax.ppermute(held, ('br', 'sub'), between + [(b, a) for a, b in between])  4.56 us
    ppermute x3, waiting for transfers between devices, shards(): lax.ppermute(x, 'br', [(i, i ^ 1 << bit) for i in range(branches)])  1.22 us
  transfers between devices with their start and end apart: 7, of which 2 were waited for; matrix products, arithmetic and copies ran while one was open for 0% of the time, Pallas kernels for 55%

commit v1 on v0

--- a/solution.py
+++ b/solution.py
@@ -1,5 +1,3 @@
-import functools
-
 import jax
 import jax.numpy as jnp
 from jax import lax
@@ -71,50 +69,58 @@
     lax.fori_loop(0, (blocks + 5) // 2, step, 0)
 
 
-def make_list(flag, source, none, height):
-    leaves, near = flag.shape
-    flags = jnp.where(flag, 1.0, 0.0)
+def make_lists(flags, source, nones, height):
+    leaves, near = source.shape
     before = lax.broadcasted_iota(jnp.int32, (near, near), 0) < lax.broadcasted_iota(jnp.int32, (near, near), 1)
-    rank = jnp.dot(flags.astype(bf16), jnp.where(before, 1.0, 0.0).astype(bf16), preferred_element_type=f32)
-    number = jnp.sum(flags, axis=1, keepdims=True).astype(jnp.int32)
-    even = (number + (number & 1)).astype(f32)
+    before = jnp.where(before, 1.0, 0.0).astype(bf16)
     above = lax.broadcasted_iota(jnp.int32, (leaves, leaves), 1) < lax.broadcasted_iota(jnp.int32, (leaves, leaves), 0)
-    start = jnp.dot(
-        jnp.where(above, 1.0, 0.0).astype(bf16),
-        jnp.broadcast_to(even, (leaves, near)).astype(bf16),
-        preferred_element_type=f32,
-    )
-    place = jnp.where(flag, (start + rank).astype(jnp.int32) + 4 * Q, -1)
-    high, low = place >> (WIDE.bit_length() - 1), place & (WIDE - 1)
-    lane = lax.broadcasted_iota(jnp.int32, (leaves, 2 * WIDE), 1)
-    leaf = lax.broadcasted_iota(jnp.int32, (leaves, 2 * WIDE), 0)
-    line = lax.broadcasted_iota(jnp.int32, (leaves, height), 1)
+    above = jnp.where(above, 1.0, 0.0).astype(bf16)
+    packed = jnp.full((leaves, near), -1, jnp.int32)
+    pairs = []
+    for k, flag in enumerate(flags):
+        ones = jnp.where(flag, 1.0, 0.0)
+        number = jnp.sum(ones, axis=1, keepdims=True).astype(jnp.int32)
+        even = (number + (number & 1)).astype(f32)
+        place = jnp.dot(ones.astype(bf16), before, preferred_element_type=f32) + jnp.dot(
+            above, jnp.broadcast_to(even, (leaves, near)).astype(bf16), preferred_element_type=f32
+        )
+        place = place.astype(jnp.int32) + (4 * Q + k * height * WIDE)
+        packed = jnp.where(flag, place * 128 + source + 1, packed)
+        pairs.append((jnp.sum(even, axis=0, keepdims=True) * 0.5).astype(jnp.int32))
+    wide = max(2 * height, 2 * WIDE)
+    lane = lax.broadcasted_iota(jnp.int32, (leaves, wide), 1)
+    leaf = lax.broadcasted_iota(jnp.int32, (leaves, wide), 0)
     left, right = [], []
     for j in range(near):
-        left.append(jnp.where(line == high[:, j : j + 1], 1.0, 0.0).astype(bf16))
-        value = jnp.where(lane < WIDE, leaf, source[:, j : j + 1] + 1)
-        right.append(jnp.where((lane & (WIDE - 1)) == low[:, j : j + 1], value, 0).astype(f32).astype(bf16))
+        entry = jnp.broadcast_to(packed[:, j : j + 1], (leaves, wide))
+        place = entry >> 7
+        left.append(jnp.where(lane == place >> (WIDE.bit_length() - 1), 1.0, 0.0).astype(bf16))
+        value = jnp.where(lane < WIDE, leaf, entry & 127)
+        right.append(jnp.where(((lane ^ place) & (WIDE - 1)) == 0, value, 0).astype(f32).astype(bf16))
     out = lax.dot_general(
         jnp.concatenate(left, axis=0),
         jnp.concatenate(right, axis=0),
         (((0,), (0,)), ((), ())),
         preferred_element_type=f32,
     ).astype(jnp.int32)
-    found = out[:, WIDE:]
-    code = out[:, :WIDE] * 256 + 2 * jnp.where(found == 0, none, found - 1)
     shape = (height, WIDE)
     last = lax.broadcasted_iota(jnp.int32, shape, 0) * WIDE + lax.broadcasted_iota(jnp.int32, shape, 1)
-    pairs = (jnp.sum(even, axis=0, keepdims=True) * 0.5).astype(jnp.int32)
-    return jnp.where(last == height * WIDE - 1, pairs, code)
+    lists = []
+    for k, none in enumerate(nones):
+        lines = slice(k * height, (k + 1) * height)
+        found = out[lines, WIDE : 2 * WIDE]
+        code = out[lines, :WIDE] * 256 + 2 * jnp.where(found == 0, none, found - 1)
+        lists.append(jnp.where(last == height * WIDE - 1, pairs[k], code))
+    return lists
 
 
 def prepare(*refs):
     fetched = 14
     sources = refs[:fetched]
-    charges, order, near_tab, far_tab = refs[fetched : fetched + 4]
+    charges, order, near_src, near_count = refs[fetched : fetched + 4]
     kept = refs[fetched + 4 : fetched + 13]
     feats, tall = refs[fetched + 13 : fetched + 15]
-    coords, near_src, near_count, wide, high, sems, coded, code_sems = refs[fetched + 15 :]
+    coords, wide, high, sems = refs[fetched + 15 :]
     copies = [
         pltpu.make_async_copy(source, dest, sems.at[i])
         for i, (source, dest) in enumerate(
@@ -122,25 +128,6 @@
         )
     ]
     for copy in copies:
-        copy.start()
-    leaves = order.shape[0]
-    first = lax.axis_index(("br", "sub")) * leaves
-    for i in (3, 4):
-        copies[i].wait()
-    near = near_src.shape[1]
-    square = (leaves, leaves)
-    diagonal = lax.broadcasted_iota(jnp.int32, square, 0) == lax.broadcasted_iota(jnp.int32, square, 1)
-    live = jnp.sum(jnp.where(diagonal, near_count[...], 0), axis=1, keepdims=True)
-    valid = lax.broadcasted_iota(jnp.int32, (leaves, near), 1) < live
-    offset = near_src[...] - first
-    here = (offset >= 0) & (offset < leaves)
-    height = coded.shape[1]
-    coded[0] = make_list(here & valid, offset, leaves, height)
-    coded[1] = make_list(jnp.logical_not(here) & valid, offset + leaves, 3 * leaves, height)
-    code_copies = [
-        pltpu.make_async_copy(coded.at[i], dest, code_sems.at[i]) for i, dest in enumerate((near_tab, far_tab))
-    ]
-    for copy in code_copies:
         copy.start()
     wide[...] = jnp.zeros_like(wide)
     high[...] = jnp.zeros_like(high)
@@ -169,22 +156,61 @@
     high[32:35, :] = r3
     high[44:45, :] = n3
     tall[...] = high[...].astype(bf16)
-    for copy in code_copies:
-        copy.wait()
-    for i in (0, 1, *range(5, fetched)):
+    for i in (0, 1, *range(3, fetched)):
         copies[i].wait()
 
 
-def turn(tall, target):
-    width = tall.shape[1]
+def turn(near_src, near_count, tall, near_tab, far_tab, target, coded, sems):
+    leaves, near = near_src.shape
+    square = (leaves, leaves)
+    diagonal = lax.broadcasted_iota(jnp.int32, square, 0) == lax.broadcasted_iota(jnp.int32, square, 1)
+    live = jnp.sum(jnp.where(diagonal, near_count[...], 0), axis=1, keepdims=True)
+    valid = lax.broadcasted_iota(jnp.int32, (leaves, near), 1) < live
+    offset = near_src[...] - lax.axis_index(("br", "sub")) * leaves
+    here = (offset >= 0) & (offset < leaves)
+    height = coded.shape[1]
+    flags = (valid & here, valid & jnp.logical_not(here))
+    source = jnp.where(here, offset, offset + leaves)
+    coded[0], coded[1] = make_lists(flags, source, (leaves, 3 * leaves), height)
+    copies = [pltpu.make_async_copy(coded.at[i], tab, sems.at[i]) for i, tab in enumerate((near_tab, far_tab))]
+    for copy in copies:
+        copy.start()
     square = (128, 128)
     one = jnp.where(
         lax.broadcasted_iota(jnp.int32, square, 0) == lax.broadcasted_iota(jnp.int32, square, 1), 1.0, 0.0
     ).astype(bf16)
-    for at in range(0, width, 128):
+    for at in range(0, tall.shape[1], 128):
         target[at : at + 128, :] = lax.dot_general(
             one, tall[:, at : at + 128], NT, preferred_element_type=f32
         ).astype(bf16)
+    for copy in copies:
+        copy.wait()
+
+
+def node_places(skeleton, node, rank):
+    both = skeleton[:, pl.ds(pl.multiple_of((node >> 1) * (2 * rank), 2 * rank), 2 * rank)]
+    return jnp.where((node & 1) == 1, both[:, rank:], both[:, :rank])
+
+
+def top_kernels(top_src, skeleton, tops, places):
+    fan = top_src.shape[0]
+    rank = tops.shape[1]
+    places[...] = jnp.zeros_like(places)
+    offset = 0
+    for level in range(3):
+        row = offset + (lax.axis_index("br") >> level)
+        places[0:3, 0:rank] = node_places(skeleton, row, rank)
+        own = places[...].T
+        kernels = []
+        for j in range(fan):
+            there = node_places(skeleton, offset + top_src[j, row], rank)
+            squared = None
+            for d in range(3):
+                gap = (there[d : d + 1, :] - own[0:rank, d : d + 1]) * scale
+                squared = gap * gap if squared is None else squared + gap * gap
+            kernels.append(profile_of(squared))
+        tops[level] = jnp.concatenate(kernels, axis=1)
+        offset += lax.axis_size("br") >> level
 
 
 def table_height(leaves, near):
@@ -218,10 +244,7 @@
             leaf = within(c - 4) * per + 2 * pair
             both = raw[1 - u][lines, :]
             coef = jnp.where(early, both[:rhs], both[rhs:])
-            turned = pltpu.roll(coef, rank, 1)
             packed[:, columns(leaf >> 1)] = coef.astype(bf16)
-            pack[rhs + FEAT :, columns(leaf)] = jnp.where(early, coef, turned).astype(bf16)
-            pack[rhs + FEAT :, columns(leaf + 1)] = jnp.where(early, turned, coef).astype(bf16)
             leaf = within(c - 3) * per + 2 * pair
             raw[u][lines, :] = lax.dot_general(
                 jnp.concatenate([pack[0:rhs, columns(leaf)], pack[0:rhs, columns(leaf + 1)]], axis=0),
@@ -235,6 +258,8 @@
 
     permute(rows, order, store, extra, hots, picks, rhs)
     half = rhs // 2
+    pack[rhs + FEAT :, : leaves * rank] = packed[:half, :]
+    pack[rhs + FEAT :, leaves * rank :] = packed[half:, :]
     total = jnp.dot(packed[...], transfer[...].reshape(leaves * rank, rank), preferred_element_type=f32)
     lifted = jnp.dot(total, branch_transfer[0].astype(f32), precision=HIGHEST)
     parent = lax.axis_index("br") // 2
@@ -295,9 +320,7 @@
     values[:, :width] = pack[0:rhs, :]
     values[:, width:] = jnp.zeros_like(values[:, width:])
     out[...] = jnp.zeros_like(out)
-    near_items(
-        tab, target, sources, values, out, scratch[:UNROLL], scratch[UNROLL:], points
-    )
+    near_items(tab, target, sources, values, out, scratch[:UNROLL], scratch[UNROLL:], points)
 
 
 def near_remote(
@@ -314,14 +337,28 @@
         to = pl.ds(pl.multiple_of(at, width), width)
         sources[:, to] = ref[rhs : rhs + FEAT, :]
         values[:, to] = ref[0:rhs, :]
-        coefs[:, to] = ref[rhs + FEAT :, :]
+    early_values = lax.broadcasted_iota(jnp.int32, (rhs, points), 1) < rank
+    half = leaves * rank
+    for window, ref in ((side, outer), (2 - side, inner), (1, pack)):
+        for i in range(leaves // 2):
+            at = i * points
+            block = jnp.concatenate(
+                [
+                    ref[rhs + FEAT :, at : at + points].astype(f32),
+                    ref[rhs + FEAT :, half + at : half + at + points].astype(f32),
+                ],
+                axis=0,
+            )
+            turned = pltpu.roll(block, rank, 1)
+            for k, twice in enumerate(((block, turned), (turned, block))):
+                to = pl.ds(pl.multiple_of((window * leaves + 2 * i + k) * points, points), points)
+                coefs[:, to] = jnp.where(early_values, *twice).astype(bf16)
     for ref in (sources, values, coefs):
         ref[:, none * points :] = jnp.zeros_like(ref[:, none * points :])
     out[...] = start[...]
     distances, kernels = scratch[:UNROLL], scratch[UNROLL:]
     near_items(tab, target, sources, values, out, distances, kernels, points)
     early = lax.broadcasted_iota(jnp.int32, (FEAT, points), 1) < rank
-    early_values = lax.broadcasted_iota(jnp.int32, (rhs, points), 1) < rank
     base = (lax.axis_index(("br", "sub")) - 1) * leaves
 
     def columns(leaf):
@@ -333,34 +370,41 @@
         return columns(jnp.where(j < far_count[leaf], far_src[j, leaf] - base, none))
 
     items = leaves // 2
+    groups = (far + 1) // 2
+    wide = groups * points
 
     def far_step(i, _):
         for u in range(UNROLL):
             item = i * UNROLL + u
             behind, last = (u - 1) % UNROLL, (u - 2) % UNROLL
-            done = jnp.maximum(item - 2, 0)
+            done = jnp.clip(item - 2, 0, items - 1)
             ahead = jnp.minimum(item, items - 1)
-            total = jnp.zeros((2 * rhs, points), f32)
-            for g in range((far + 1) // 2):
-                part = slice(g * points, (g + 1) * points)
-                pair = []
-                for leaf in (2 * done, 2 * done + 1):
-                    one, two = picked(leaf, 2 * g), picked(leaf, 2 * g + 1)
-                    pair.append(jnp.where(early_values, coefs[:, one], coefs[:, two]))
-                total += lax.dot_general(
-                    jnp.concatenate(pair, axis=0), kernels[last][:, part], NT, preferred_element_type=f32
-                )
-                kernels[behind][:, part] = profile_of(distances[behind][:, part]).astype(bf16)
-                for k in range(2):
-                    leaf = 2 * ahead + k
+            pairs = [[], []]
+            for k in range(2):
+                for g in range(groups):
+                    one, two = picked(2 * done + k, 2 * g), picked(2 * done + k, 2 * g + 1)
+                    pairs[k].append(jnp.where(early_values, coefs[:, one], coefs[:, two]))
+            total = lax.dot_general(
+                jnp.concatenate([jnp.concatenate(pair, axis=1) for pair in pairs], axis=0),
+                kernels[last][:, :wide],
+                NT,
+                preferred_element_type=f32,
+            )
+            for k in range(2):
+                lines = slice(k * rank, (k + 1) * rank)
+                kernels[behind][lines, :wide] = profile_of(distances[behind][lines, :wide]).astype(bf16)
+                leaf = 2 * ahead + k
+                places = []
+                for g in range(groups):
                     one, two = picked(leaf, 2 * g), picked(leaf, 2 * g + 1)
                     turned = pltpu.roll(sources[:, two].astype(f32), rank, 1)
-                    both = jnp.where(early, sources[:, one].astype(f32), turned).astype(bf16)
-                    distances[u][k * rank : (k + 1) * rank, part] = jnp.dot(
-                        target[pl.ds(pl.multiple_of(leaf * points, points), rank), :],
-                        jnp.concatenate([both, both, both], axis=0),
-                        preferred_element_type=f32,
-                    )
+                    places.append(jnp.where(early, sources[:, one].astype(f32), turned).astype(bf16))
+                places = jnp.concatenate(places, axis=1)
+                distances[u][lines, :wide] = jnp.dot(
+                    target[pl.ds(pl.multiple_of(leaf * points, points), rank), :],
+                    jnp.concatenate([places] * 3, axis=0),
+                    preferred_element_type=f32,
+                )
             field[:, columns(done)] = jnp.where(early_values, total[:rhs], total[rhs:])
         return 0
 
@@ -368,7 +412,7 @@
 
 
 def downward(
-    top_src, top_count, mine, theirs, skeleton, near, field, basis, transfer, branch_transfer, upper_transfer, out, places, every
+    top_src, top_count, mine, theirs, tops, near, field, basis, transfer, branch_transfer, upper_transfer, out, every, halves
 ):
     rhs = near.shape[0]
     leaves, rank, points = basis.shape
@@ -379,11 +423,6 @@
     fan = top_src.shape[0]
     every[0 : mine.shape[0], :] = mine[...]
     every[mine.shape[0] :, :] = theirs[...]
-    places[...] = jnp.zeros_like(places)
-
-    def node_places(node):
-        both = skeleton[:, pl.ds(pl.multiple_of((node >> 1) * (2 * rank), 2 * rank), 2 * rank)]
-        return jnp.where((node & 1) == 1, both[:, rank:], both[:, :rank])
 
     def coefficients(level, node):
         total = None
@@ -405,22 +444,14 @@
     for level in range(3):
         node = branch >> level
         row = offset + node
-        places[0:3, 0:rank] = node_places(row)
-        own = places[...].T
-        kernels, coefs = [], []
+        coefs = []
         for j in range(fan):
             source = top_src[j, row]
-            there = node_places(offset + source)
-            squared = None
-            for d in range(3):
-                gap = (there[d : d + 1, :] - own[0:rank, d : d + 1]) * scale
-                squared = gap * gap if squared is None else squared + gap * gap
-            kernels.append(profile_of(squared))
             coefs.append(jnp.where(j < top_count[row], coefficients(level, source), 0.0))
         fields.append(
             lax.dot_general(
                 jnp.concatenate(coefs, axis=1),
-                jnp.concatenate(kernels, axis=1),
+                tops[level],
                 NT,
                 precision=HIGHEST,
                 preferred_element_type=f32,
@@ -434,19 +465,19 @@
         down_one, branch_transfer[0].astype(f32), NT, precision=HIGHEST, preferred_element_type=f32
     )
     down_zero = down_zero.astype(bf16)
-    lane = lax.broadcasted_iota(jnp.int32, (rhs, 2 * rank), 1)
+    down = field[...] + lax.dot_general(
+        down_zero, transfer[...].reshape(leaves * rank, rank), NT, preferred_element_type=f32
+    )
+    early = (lax.broadcasted_iota(jnp.int32, down.shape, 1) & (2 * rank - 1)) < rank
+    halves[0:rhs, :] = jnp.where(early, down, 0.0).astype(bf16)
+    halves[rhs:, :] = jnp.where(early, 0.0, down).astype(bf16)
     for i in range(leaves // 2):
         at = 2 * i * rank
-        down = field[:, at : at + 2 * rank] + lax.dot_general(
-            down_zero,
-            transfer[2 * i : 2 * i + 2].reshape(2 * rank, rank),
-            NT,
+        value = jnp.dot(
+            halves[:, at : at + 2 * rank],
+            basis[2 * i : 2 * i + 2].reshape(2 * rank, points),
             preferred_element_type=f32,
         )
-        both = jnp.concatenate(
-            [jnp.where(lane < rank, down, 0.0), jnp.where(lane < rank, 0.0, down)], axis=0
-        ).astype(bf16)
-        value = jnp.dot(both, basis[2 * i : 2 * i + 2].reshape(2 * rank, points), preferred_element_type=f32)
         for k in range(2):
             col = (2 * i + k) * points
             out[:, col : col + points] = near[:, col : col + points] + value[k * rhs : (k + 1) * rhs]
@@ -487,26 +518,21 @@
         far_src.T, far_count, top_src.T, top_count,
     ]
     (
-        own, order, near_tab, far_tab,
+        own, order, near_src, near_count,
         leaf_basis, leaf_transfer, branch_transfer, upper_transfer, top_skeleton,
         far_src, far_count, top_src, top_count,
         feats, tall,
     ) = pl.pallas_call(
         prepare,
-        out_shape=(like(charges), like(order), shape((height, WIDE), jnp.int32), shape((height, WIDE), jnp.int32))
-        + tuple(like(x) for x in fetched[5:])
+        out_shape=tuple(like(x) for i, x in enumerate(fetched) if i != 2)
         + (shape((FEAT, width), bf16), shape((3 * FEAT, width), bf16)),
         in_specs=[HBM] * len(fetched),
-        out_specs=(VMEM, VMEM, SMEM, SMEM) + (VMEM,) * 5 + (SMEM,) * 4 + (VMEM, VMEM),
+        out_specs=(VMEM,) * 9 + (SMEM,) * 4 + (VMEM, VMEM),
         scratch_shapes=[
             pltpu.VMEM(coords.shape, f32),
-            pltpu.VMEM(near_src.shape, jnp.int32),
-            pltpu.VMEM((1, leaves), jnp.int32),
             pltpu.VMEM((FEAT, width), f32),
             pltpu.VMEM((3 * FEAT, width), f32),
             pltpu.SemaphoreType.DMA((len(fetched),)),
-            pltpu.VMEM((2, height, WIDE), jnp.int32),
-            pltpu.SemaphoreType.DMA((2,)),
         ],
         compiler_params=params,
         cost_estimate=cost(2),
@@ -516,7 +542,7 @@
     pack, up = pl.pallas_call(
         upward,
         out_shape=(
-            shape((2 * rhs + FEAT, width), bf16),
+            shape((rhs + FEAT + rhs // 2, width), bf16),
             shape((rhs + rhs // 2, 2 * rank), f32),
         ),
         in_specs=[VMEM] * 8,
@@ -535,20 +561,33 @@
         own, partner, order, feats,
         leaf_basis, leaf_transfer, branch_transfer, upper_transfer,
     )
-    target = pl.pallas_call(
+    near_tab, far_tab, target = pl.pallas_call(
         turn,
-        out_shape=shape((width, 3 * FEAT), bf16),
-        in_specs=[VMEM],
+        out_shape=(shape((height, WIDE), jnp.int32),) * 2 + (shape((width, 3 * FEAT), bf16),),
+        in_specs=[VMEM] * 3,
+        out_specs=(SMEM, SMEM, VMEM),
+        scratch_shapes=[pltpu.VMEM((2, height, WIDE), jnp.int32), pltpu.SemaphoreType.DMA((2,))],
+        compiler_params=params,
+        cost_estimate=cost(2),
+        name="turn",
+    )(near_src, near_count, tall)
+    tops = pl.pallas_call(
+        top_kernels,
+        out_shape=shape((3, rank, top_src.shape[0] * rank), f32),
+        in_specs=[SMEM, VMEM],
         out_specs=VMEM,
+        scratch_shapes=[pltpu.VMEM((8, 128), f32)],
         compiler_params=params,
         cost_estimate=cost(1),
-        name="turn",
-    )(tall)
-    up = up + lax.ppermute(up, "sub", swap)
+        name="top_kernels",
+    )(top_src, top_skeleton)
+    exchange = lambda x, bit: lax.ppermute(x, "br", [(i, i ^ (1 << bit)) for i in range(branches)])
+    other, near_tab, far_tab, target = lax.optimization_barrier(
+        (lax.ppermute(up, "sub", swap), near_tab, far_tab, target)
+    )
+    mine = up + other
+    theirs, held, tops = lax.optimization_barrier((exchange(mine, 0), pack, tops))
     between = [(2 * j + 1, 2 * j + 2) for j in range(branches - 1)]
-    up, held = lax.optimization_barrier((up, pack))
-    exchange = lambda x, bit: lax.ppermute(x, "br", [(i, i ^ (1 << bit)) for i in range(branches)])
-    theirs, held = lax.optimization_barrier((exchange(up, 0), held))
     outer = lax.ppermute(held, ("br", "sub"), between + [(b, a) for a, b in between])
     inner = lax.ppermute(held, "sub", swap)
     pipeline = [pltpu.VMEM((points, 2 * Q * points), f32)] * UNROLL + [
@@ -567,11 +606,10 @@
             ]
             + pipeline,
             compiler_params=params,
-            cost_estimate=cost(11),
+            cost_estimate=cost(6),
             name="near_local",
         )(near_tab, held, target)
 
-    mine = up
     for bit in range(1, branches.bit_length() - 1):
         mine = jnp.concatenate([mine, theirs], axis=0)
         theirs = exchange(mine, bit)
@@ -591,21 +629,21 @@
         compiler_params=params,
         cost_estimate=cost(14),
         name="near_remote",
-    )(far_tab, far_src, far_count, outer, inner, pack, target, start)
+    )(far_tab, far_src, far_count, outer, inner, held, target, start)
     return pl.pallas_call(
         downward,
         out_shape=shape((rhs, width), f32),
         in_specs=[SMEM, SMEM] + [VMEM] * 9,
         out_specs=VMEM,
         scratch_shapes=[
-            pltpu.VMEM((8, 128), f32),
             pltpu.VMEM((branches * up.shape[0], 2 * rank), f32),
+            pltpu.VMEM((2 * rhs, leaves * rank), bf16),
         ],
         compiler_params=params,
         cost_estimate=cost(4),
         name="downward",
     )(
-        top_src, top_count, mine, theirs, top_skeleton, both, field,
+        top_src, top_count, mine, theirs, tops, both, field,
         leaf_basis, leaf_transfer, branch_transfer, upper_transfer,
     )
 

time: 56.5 us -> 52.5 us (0.929)
  Pallas kernels: 43 us -> 39.6 us
  waiting for transfers between devices: 2.08 us -> 0.02 us
  starting transfers between devices: 11.4 us -> 12.7 us
    pallas_call x1, Pallas kernels: 5.25 us -> 2.73 us  [shards(): pl.pallas_call(downward, out_shape=shape((rhs, width), f32), in_specs=[SM...]
    ppermute x3, waiting for transfers between devices: 1.22 us -> 0.01 us  [shards(): lax.ppermute(x, 'br', [(i, i ^ 1 << bit) for i in range(branches)])]
    ppermute x3, starting transfers between devices: 6.29 us -> 7.25 us  [shards(): lax.ppermute(x, 'br', [(i, i ^ 1 << bit) for i in range(branches)])]
    pallas_call x1, Pallas kernels: 14.9 us -> 14.1 us  [shards(): pl.pallas_call(near_remote, out_shape=(shape((rhs, width), f32), shape((r...]
    ppermute x1, waiting for transfers between devices: 0.85 us -> 0.01 us  [shards(): lax.ppermute(up, 'sub', swap)]
    pallas_call x1, Pallas kernels: 10.8 us -> 10.1 us  [local(): pl.pallas_call(near_local, out_shape=shape((rhs, width), f32), in_specs=[...]
    pallas_call x3 -> x4, Pallas kernels: 12.1 us -> 12.6 us  [the longest x1 6.02 us: shards(): pl.pallas_call(upward, out_shape=(shape((rhs + FEAT + rhs // 2, width), b...]
  transfers between devices with their start and end apart: 7 -> 7, of which waited for: 2 -> 0; matrix products, arithmetic and copies ran while one was open for 0% -> 0% of each run, Pallas kernels for 55% -> 59%
where the time goes in v1:
time: 52.5 us; the launch traced here: 52.4 us
  Pallas kernels  39.6 us (75%)
  starting transfers between devices  12.7 us (24%)
    pallas_call x1, Pallas kernels, shards(): pl.pallas_call(near_remote, out_shape=(shape((rhs, width), f32), shape((r...  14.1 us
    pallas_call x1, Pallas kernels, local(): pl.pallas_call(near_local, out_shape=shape((rhs, width), f32), in_specs=[...  10.1 us
    ppermute x3, starting transfers between devices, shards(): lax.ppermute(x, 'br', [(i, i ^ 1 << bit) for i in range(branches)])  7.25 us
    pallas_call x1, Pallas kernels, shards(): pl.pallas_call(upward, out_shape=(shape((rhs + FEAT + rhs // 2, width), b...  6.02 us
    ppermute x1, starting transfers between devices, shards(): lax.ppermute(held, ('br', 'sub'), between + [(b, a) for a, b in between])  4.82 us
    pallas_call x1, Pallas kernels, shards(): pl.pallas_call(turn, out_shape=(shape((height, WIDE), jnp.int32),) * 2 +...  3.09 us
    pallas_call x1, Pallas kernels, shards(): pl.pallas_call(downward, out_shape=shape((rhs, width), f32), in_specs=[SM...  2.73 us
    pallas_call x1, Pallas kernels, shards(): pl.pallas_call(prepare, out_shape=tuple((like(x) for i, x in enumerate(fe...  2.27 us
  transfers between devices with their start and end apart: 7, of which 0 were waited for; matrix products, arithmetic and copies ran while one was open for 0% of the time, Pallas kernels for 59%

profile of v1, /device:TPU:1, one launch (start us, length us, event | category | flops | bytes accessed | tf_op | source)
XLA Modules:
  0.0 52.4 jit_solution(7514933050011304594)
XLA Ops:
  0.0 0.1 collective-permute-start
  0.1 2.3 %prepare.1 = (bf16[32,4096]{1,0:T(8,128)(2,1)S(1)}, s32[32,128]{1,0:T(8,128)S(1)}, s32[32,27]{1,0:T(8,128)S(1)}, s32[1,32]{1,0:T(1,128)S(1)}, bf16[32,64,128]{2,...) custom-call(bf16[32,4096]{1,0:T(8,128)(2,1)} %refs_0_.1, ...), custom_call_target="tpu_custom_call" | custom-call | flops 2000000 | bytes 6000000 | tf_op jit(solution)/shard_map/prepare/pallas_call | solution.py:525
  2.3 0.0 collective-permute-done.partner
  2.3 6.0 %upward.1 = (bf16[64,4096]{1,0:T(8,128)(2,1)S(1)}, f32[48,128]{1,0:T(8,128)S(1)}) custom-call(bf16[32,4096]{1,0:T(8,128)(2,1)S(1)} %get-tuple-element.38.charges, bf16[32,4096]{1,0:T(8,128)(2,1)S(1)} %collective-permute-done.partner, s32[32,128]{1,0:T(8,128)S(1)} %get-tuple-element.39.order, bf16[16,4096]{1,0:T(8,128)(2,1)S(1)} %get-tuple-element.40.feats, ...), custom_call_target="tpu_custom_call" | custom-call | flops 6000000 | bytes 18000000 | tf_op jit(solution)/shard_map/upward/pallas_call | solution.py:542
  8.4 0.5 collective-permute-start.1
  8.8 3.1 %turn.1 = (s32[32,32]{1,0:T(8,128)S(1)}, s32[32,32]{1,0:T(8,128)S(1)}, bf16[4096,48]{1,0:T(8,128)(2,1)S(1)}) custom-call(s32[32,27]{1,0:T(8,128)S(1)} %get-tuple-element.46.near_src, s32[1,32]{1,0:T(1,128)S(1)} %get-tuple-element.47.near_count, bf16[48,4096]{1,0:T(8,128)(2,1)S(1)} %get-tuple-element.48.tall), custom_call_target="tpu_custom_call" | custom-call | flops 2000000 | bytes 6000000 | tf_op jit(solution)/shard_map/turn/pallas_call | solution.py:564
  11.9 0.0 collective-permute-done.1
  12.0 2.3 %collective-permute-start.2 = (f32[48,128]{1,0:T(8,128)S(1)}, f32[48,128]{1,0:T(8,128)S(1)}, u32[]{:S(2)}, u32[]{:S(2)}) collective-permute-start(f32[48,128]{1,0:T(8,128)S(1)} %add.3), channel_id=1, source_target_pairs={{0,2},{2,0},{4,6},{6,4},{8,10},{10,8},{12,14},{14,12},{1,3},{3,1},... | collective-permute-start | bytes 73736 | tf_op jit(solution)/shard_map/ppermute | solution.py:584
  14.2 1.3 %top_kernels.1.tops = f32[3,64,384]{2,1,0:T(8,128)S(1)} custom-call(s32[6,14]{1,0:T(8,128)S(1)} %get-tuple-element.36.top_src, f32[3,896]{1,0:T(4,128)S(1)} %get-tuple-element.54.skeleton), custom_call_target="tpu_custom_call" | custom-call | flops 1000000 | bytes 3000000 | tf_op jit(solution)/shard_map/top_kernels/pallas_call | solution.py:574
  15.5 0.0 collective-permute-done.2
  15.5 4.8 %collective-permute-start.5 = (bf16[64,4096]{1,0:T(8,128)(2,1)S(1)}, bf16[64,4096]{1,0:T(8,128)(2,1)S(1)}, u32[]{:S(2)}, u32[]{:S(2)}) collective-permute-start(bf16[64,4096]{1,0:T(8,128)(2,1)S(1)} %get-tuple-element.57.pack), channel_id=1, source_target_pairs={{1,2},{3,4},{5,6},{7,8},{9,10},{11,12},{13,14},{2,1},{4,3},{6,5},{... | collective-permute-start | bytes 1572872 | tf_op jit(solution)/shard_map/ppermute | solution.py:591
  20.4 0.1 collective-permute-start.6
  20.4 1.4 %collective-permute-start.3 = (f32[96,128]{1,0:T(8,128)S(1)}, f32[96,128]{1,0:T(8,128)S(1)}, u32[]{:S(2)}, u32[]{:S(2)}) collective-permute-start(f32[96,128]{1,0:T(8,128)S(1)} %pad_maximum_fusion.1), channel_id=1, source_target_pairs={{0,4},{2,6},{4,0},{6,2},{8,12},{10,14},{12,8},{14,10},{1,5},{3,7},... | collective-permute-start | bytes 147464 | tf_op jit(solution)/shard_map/ppermute | solution.py:584
  21.8 10.1 %near_local.1.start = f32[32,4096]{1,0:T(8,128)S(1)} custom-call(s32[32,32]{1,0:T(8,128)S(1)} %get-tuple-element.56.tab, bf16[64,4096]{1,0:T(8,128)(2,1)S(1)} %get-tuple-element.57.pack, bf16[4096,48]{1,0:T(8,128)(2,1)S(1)} %get-tuple-element.58.target), custom_call_target="tpu_custom_call" | custom-call | flops 6000000 | bytes 18000000 | tf_op jit(solution)/shard_map/near_local/pallas_call | solution.py:598
  31.9 0.0 collective-permute-done.3
  32.0 3.6 %collective-permute-start.4 = (f32[192,128]{1,0:T(8,128)S(1)}, f32[192,128]{1,0:T(8,128)S(1)}, u32[]{:S(2)}, u32[]{:S(2)}) collective-permute-start(f32[192,128]{1,0:T(8,128)S(1)} %pad_maximum_fusion.mine), channel_id=1, source_target_pairs={{0,8},{2,10},{4,12},{6,14},{8,0},{10,2},{12,4},{14,6},{1,9},{3,11}... | collective-permute-start | bytes 294920 | tf_op jit(solution)/shard_map/ppermute | solution.py:584
  35.6 0.0 collective-permute-done.5.outer
  35.6 0.0 collective-permute-done.6.inner
  35.6 14.1 %near_remote.1 = (f32[32,4096]{1,0:T(8,128)S(1)}, f32[32,2048]{1,0:T(8,128)S(1)}) custom-call(s32[32,32]{1,0:T(8,128)S(1)} %get-tuple-element.61.tab, s32[6,32]{1,0:T(8,128)S(1)} %get-tuple-element.62.far_src, s32[32]{0:T(128)S(1)} %get-tuple-element.63.far_count, bf16[64,4096]{1,0:T(8,128)(2,1)S(1)} %collective-permute-done.5.outer, ...), custom_call_target="tpu_custom_call" | custom-call | flops 14000000 | bytes 42000000 | tf_op jit(solution)/shard_map/near_remote/pallas_call | solution.py:618
  49.7 0.0 collective-permute-done.4.theirs
  49.7 2.7 %downward.1 = f32[32,4096]{1,0:T(8,128)} custom-call(s32[6,14]{1,0:T(8,128)S(1)} %get-tuple-element.36.top_src, s32[14]{0:T(128)S(1)} %get-tuple-element.37.top_count, f32[192,128]{1,0:T(8,128)S(1)} %pad_maximum_fusion.mine, f32[192,128]{1,0:T(8,128)S(1)} %collective-permute-done.4.theirs, f32[3,64,384]{2,1,0:T(8,128)S(1)} %top_kernels.1.tops, ...), custom_call_target="tpu_custom_call" | custom-call | flops 4000000 | bytes 12000000 | tf_op jit(solution)/shard_map/downward/pallas_call | solution.py:633
  (3 shorter events, 0.0 us)
Async XLA Ops:
  0.0 2.3 %collective-permute-start = (bf16[32,4096]{1,0:T(8,128)(2,1)}, bf16[32,4096]{1,0:T(8,128)(2,1)S(1)}, u32[]{:S(2)}, u32[]{:S(2)}) collective-permute-start(bf16[32,4096]{1,0:T(8,128)(2,1)} %refs_0_.1), channel_id=1, source_target_pairs={{0,1},{1,0},{2,3},{3,2},{4,5},{5,4},{6,7},{7,6},{8,9},{9,8},{10,11... | collective-permute-start | bytes 786440 | tf_op jit(solution)/shard_map/ppermute | solution.py:514
  8.4 3.6 %collective-permute-start.1 = (f32[48,128]{1,0:T(8,128)S(1)}, f32[48,128]{1,0:T(8,128)S(1)}, u32[]{:S(2)}, u32[]{:S(2)}) collective-permute-start(f32[48,128]{1,0:T(8,128)S(1)} %get-tuple-element.45), channel_id=1, source_target_pairs={{0,1},{1,0},{2,3},{3,2},{4,5},{5,4},{6,7},{7,6},{8,9},{9,8},{10,11... | collective-permute-start | bytes 73736 | tf_op jit(solution)/shard_map/ppermute | solution.py:586
  12.0 3.6 %collective-permute-start.2 = (f32[48,128]{1,0:T(8,128)S(1)}, f32[48,128]{1,0:T(8,128)S(1)}, u32[]{:S(2)}, u32[]{:S(2)}) collective-permute-start(f32[48,128]{1,0:T(8,128)S(1)} %add.3), channel_id=1, source_target_pairs={{0,2},{2,0},{4,6},{6,4},{8,10},{10,8},{12,14},{14,12},{1,3},{3,1},... | collective-permute-start | bytes 73736 | tf_op jit(solution)/shard_map/ppermute | solution.py:584
  15.5 20.1 %collective-permute-start.5 = (bf16[64,4096]{1,0:T(8,128)(2,1)S(1)}, bf16[64,4096]{1,0:T(8,128)(2,1)S(1)}, u32[]{:S(2)}, u32[]{:S(2)}) collective-permute-start(bf16[64,4096]{1,0:T(8,128)(2,1)S(1)} %get-tuple-element.57.pack), channel_id=1, source_target_pairs={{1,2},{3,4},{5,6},{7,8},{9,10},{11,12},{13,14},{2,1},{4,3},{6,5},{... | collective-permute-start | bytes 1572872 | tf_op jit(solution)/shard_map/ppermute | solution.py:591
  20.4 15.2 %collective-permute-start.6 = (bf16[64,4096]{1,0:T(8,128)(2,1)S(1)}, bf16[64,4096]{1,0:T(8,128)(2,1)S(1)}, u32[]{:S(2)}, u32[]{:S(2)}) collective-permute-start(bf16[64,4096]{1,0:T(8,128)(2,1)S(1)} %get-tuple-element.57.pack), channel_id=1, source_target_pairs={{0,1},{1,0},{2,3},{3,2},{4,5},{5,4},{6,7},{7,6},{8,9},{9,8},{10,11... | collective-permute-start | bytes 1572872 | tf_op jit(solution)/shard_map/ppermute | solution.py:592
  20.4 11.5 %collective-permute-start.3 = (f32[96,128]{1,0:T(8,128)S(1)}, f32[96,128]{1,0:T(8,128)S(1)}, u32[]{:S(2)}, u32[]{:S(2)}) collective-permute-start(f32[96,128]{1,0:T(8,128)S(1)} %pad_maximum_fusion.1), channel_id=1, source_target_pairs={{0,4},{2,6},{4,0},{6,2},{8,12},{10,14},{12,8},{14,10},{1,5},{3,7},... | collective-permute-start | bytes 147464 | tf_op jit(solution)/shard_map/ppermute | solution.py:584
  32.0 17.7 %collective-permute-start.4 = (f32[192,128]{1,0:T(8,128)S(1)}, f32[192,128]{1,0:T(8,128)S(1)}, u32[]{:S(2)}, u32[]{:S(2)}) collective-permute-start(f32[192,128]{1,0:T(8,128)S(1)} %pad_maximum_fusion.mine), channel_id=1, source_target_pairs={{0,8},{2,10},{4,12},{6,14},{8,0},{10,2},{12,4},{14,6},{1,9},{3,11}... | collective-permute-start | bytes 294920 | tf_op jit(solution)/shard_map/ppermute | solution.py:584

commit v2 on v1

--- a/solution.py
+++ b/solution.py
@@ -38,7 +38,7 @@
     per = CHUNK // order.shape[1]
     groups = rows.shape[0] // rhs
     blocks = order.shape[0] // per
-    cuts = 8
+    cuts = 4
 
     def within(c):
         return jnp.clip(c, 0, blocks - 1)
@@ -374,8 +374,8 @@
     wide = groups * points
 
     def far_step(i, _):
-        for u in range(UNROLL):
-            item = i * UNROLL + u
+        for u in range(2 * UNROLL):
+            item = 2 * i * UNROLL + u
             behind, last = (u - 1) % UNROLL, (u - 2) % UNROLL
             done = jnp.clip(item - 2, 0, items - 1)
             ahead = jnp.minimum(item, items - 1)
@@ -400,7 +400,7 @@
                     turned = pltpu.roll(sources[:, two].astype(f32), rank, 1)
                     places.append(jnp.where(early, sources[:, one].astype(f32), turned).astype(bf16))
                 places = jnp.concatenate(places, axis=1)
-                distances[u][lines, :wide] = jnp.dot(
+                distances[u % UNROLL][lines, :wide] = jnp.dot(
                     target[pl.ds(pl.multiple_of(leaf * points, points), rank), :],
                     jnp.concatenate([places] * 3, axis=0),
                     preferred_element_type=f32,
@@ -408,7 +408,7 @@
             field[:, columns(done)] = jnp.where(early_values, total[:rhs], total[rhs:])
         return 0
 
-    lax.fori_loop(0, (items + 2 + UNROLL - 1) // UNROLL, far_step, 0)
+    lax.fori_loop(0, (items + 2 + 2 * UNROLL - 1) // (2 * UNROLL), far_step, 0)
 
 
 def downward(
@@ -571,6 +571,13 @@
         cost_estimate=cost(2),
         name="turn",
     )(near_src, near_count, tall)
+    exchange = lambda x, bit: lax.ppermute(x, "br", [(i, i ^ (1 << bit)) for i in range(branches)])
+    other, near_tab, far_tab, target = lax.optimization_barrier(
+        (lax.ppermute(up, "sub", swap), near_tab, far_tab, target)
+    )
+    mine = up + other
+    theirs = exchange(mine, 0)
+    mine, top_skeleton = lax.optimization_barrier((mine, top_skeleton))
     tops = pl.pallas_call(
         top_kernels,
         out_shape=shape((3, rank, top_src.shape[0] * rank), f32),
@@ -581,14 +588,10 @@
         cost_estimate=cost(1),
         name="top_kernels",
     )(top_src, top_skeleton)
-    exchange = lambda x, bit: lax.ppermute(x, "br", [(i, i ^ (1 << bit)) for i in range(branches)])
-    other, near_tab, far_tab, target = lax.optimization_barrier(
-        (lax.ppermute(up, "sub", swap), near_tab, far_tab, target)
-    )
-    mine = up + other
-    theirs, held, tops = lax.optimization_barrier((exchange(mine, 0), pack, tops))
+    held, tops = lax.optimization_barrier((pack, tops))
     between = [(2 * j + 1, 2 * j + 2) for j in range(branches - 1)]
     outer = lax.ppermute(held, ("br", "sub"), between + [(b, a) for a, b in between])
+    mine, theirs, held = lax.optimization_barrier((mine, theirs, held))
     inner = lax.ppermute(held, "sub", swap)
     pipeline = [pltpu.VMEM((points, 2 * Q * points), f32)] * UNROLL + [
         pltpu.VMEM((points, 2 * Q * points), bf16)

time: 52.5 us -> 50.4 us (0.960)
  the two profiles are of different devices: /device:TPU:1 before, /device:TPU:15 now
where the time goes in v2:
time: 50.4 us; the launch traced here: 49.9 us
  Pallas kernels  39.4 us (78%)
  starting transfers between devices  10.3 us (20%)
    pallas_call x1, Pallas kernels, shards(): pl.pallas_call(near_remote, out_shape=(shape((rhs, width), f32), shape((r...  14.3 us
    pallas_call x1, Pallas kernels, local(): pl.pallas_call(near_local, out_shape=shape((rhs, width), f32), in_specs=[...  10.1 us
    pallas_call x1, Pallas kernels, shards(): pl.pallas_call(upward, out_shape=(shape((rhs + FEAT + rhs // 2, width), b...  5.62 us
    ppermute x1, starting transfers between devices, shards(): lax.ppermute(held, ('br', 'sub'), between + [(b, a) for a, b in between])  4.81 us
    ppermute x3, starting transfers between devices, shards(): lax.ppermute(x, 'br', [(i, i ^ 1 << bit) for i in range(branches)])  4.78 us
    pallas_call x1, Pallas kernels, shards(): pl.pallas_call(turn, out_shape=(shape((height, WIDE), jnp.int32),) * 2 +...  3.1 us
    pallas_call x1, Pallas kernels, shards(): pl.pallas_call(downward, out_shape=shape((rhs, width), f32), in_specs=[SM...  2.73 us
    pallas_call x1, Pallas kernels, shards(): pl.pallas_call(prepare, out_shape=tuple((like(x) for i, x in enumerate(fe...  2.27 us
  transfers between devices with their start and end apart: 7, of which 0 were waited for; matrix products, arithmetic and copies ran while one was open for 0% of the time, Pallas kernels for 62%

profile of v2, /device:TPU:15, one launch (start us, length us, event | category | flops | bytes accessed | tf_op | source)
XLA Modules:
  0.0 49.9 jit_solution(10449793742773301502)
XLA Ops:
  0.0 0.7 %collective-permute-start = (bf16[32,4096]{1,0:T(8,128)(2,1)}, bf16[32,4096]{1,0:T(8,128)(2,1)S(1)}, u32[]{:S(2)}, u32[]{:S(2)}) collective-permute-start(bf16[32,4096]{1,0:T(8,128)(2,1)} %refs_0_.1), channel_id=1, source_target_pairs={{0,1},{1,0},{2,3},{3,2},{4,5},{5,4},{6,7},{7,6},{8,9},{9,8},{10,11... | collective-permute-start | bytes 786440 | tf_op jit(solution)/shard_map/ppermute | solution.py:514
  0.7 2.3 %prepare.1 = (bf16[32,4096]{1,0:T(8,128)(2,1)S(1)}, s32[32,128]{1,0:T(8,128)S(1)}, s32[32,27]{1,0:T(8,128)S(1)}, s32[1,32]{1,0:T(1,128)S(1)}, bf16[32,64,128]{2,...) custom-call(bf16[32,4096]{1,0:T(8,128)(2,1)} %refs_0_.1, ...), custom_call_target="tpu_custom_call" | custom-call | flops 2000000 | bytes 6000000 | tf_op jit(solution)/shard_map/prepare/pallas_call | solution.py:525
  3.0 0.0 collective-permute-done.partner
  3.0 5.6 %upward.1 = (bf16[64,4096]{1,0:T(8,128)(2,1)S(1)}, f32[48,128]{1,0:T(8,128)S(1)}) custom-call(bf16[32,4096]{1,0:T(8,128)(2,1)S(1)} %get-tuple-element.42.charges, bf16[32,4096]{1,0:T(8,128)(2,1)S(1)} %collective-permute-done.partner, s32[32,128]{1,0:T(8,128)S(1)} %get-tuple-element.43.order, bf16[16,4096]{1,0:T(8,128)(2,1)S(1)} %get-tuple-element.44.feats, ...), custom_call_target="tpu_custom_call" | custom-call | flops 6000000 | bytes 18000000 | tf_op jit(solution)/shard_map/upward/pallas_call | solution.py:542
  8.6 0.0 collective-permute-start.1
  8.6 3.1 %turn.1 = (s32[32,32]{1,0:T(8,128)S(1)}, s32[32,32]{1,0:T(8,128)S(1)}, bf16[4096,48]{1,0:T(8,128)(2,1)S(1)}) custom-call(s32[32,27]{1,0:T(8,128)S(1)} %get-tuple-element.50.near_src, s32[1,32]{1,0:T(1,128)S(1)} %get-tuple-element.51.near_count, bf16[48,4096]{1,0:T(8,128)(2,1)S(1)} %get-tuple-element.52.tall), custom_call_target="tpu_custom_call" | custom-call | flops 2000000 | bytes 6000000 | tf_op jit(solution)/shard_map/turn/pallas_call | solution.py:564
  11.7 0.0 collective-permute-done.1
  11.7 0.3 collective-permute-start.2
  12.1 1.3 %top_kernels.1.tops = f32[3,64,384]{2,1,0:T(8,128)S(1)} custom-call(s32[6,14]{1,0:T(8,128)S(1)} %get-tuple-element.40.top_src, f32[3,896]{1,0:T(4,128)S(1)} %get-tuple-element.60.skeleton), custom_call_target="tpu_custom_call" | custom-call | flops 1000000 | bytes 3000000 | tf_op jit(solution)/shard_map/top_kernels/pallas_call | solution.py:581
  13.3 4.8 %collective-permute-start.5 = (bf16[64,4096]{1,0:T(8,128)(2,1)S(1)}, bf16[64,4096]{1,0:T(8,128)(2,1)S(1)}, u32[]{:S(2)}, u32[]{:S(2)}) collective-permute-start(bf16[64,4096]{1,0:T(8,128)(2,1)S(1)} %get-tuple-element.65.pack), channel_id=1, source_target_pairs={{1,2},{3,4},{5,6},{7,8},{9,10},{11,12},{13,14},{2,1},{4,3},{6,5},{... | collective-permute-start | bytes 1572872 | tf_op jit(solution)/shard_map/ppermute | solution.py:593
  18.2 0.0 collective-permute-done.2
  18.2 0.1 collective-permute-start.6
  18.3 0.2 collective-permute-start.3
  18.5 10.1 %near_local.1.start = f32[32,4096]{1,0:T(8,128)S(1)} custom-call(s32[32,32]{1,0:T(8,128)S(1)} %get-tuple-element.64.tab, bf16[64,4096]{1,0:T(8,128)(2,1)S(1)} %get-tuple-element.65.pack, bf16[4096,48]{1,0:T(8,128)(2,1)S(1)} %get-tuple-element.66.target), custom_call_target="tpu_custom_call" | custom-call | flops 6000000 | bytes 18000000 | tf_op jit(solution)/shard_map/near_local/pallas_call | solution.py:601
  28.6 0.0 collective-permute-done.3
  28.6 4.2 %collective-permute-start.4 = (f32[192,128]{1,0:T(8,128)S(1)}, f32[192,128]{1,0:T(8,128)S(1)}, u32[]{:S(2)}, u32[]{:S(2)}) collective-permute-start(f32[192,128]{1,0:T(8,128)S(1)} %constant_dynamic-update-slice_fusion.mine), channel_id=1, source_target_pairs={{0,8},{2,10},{4,12},{6,14},{8,0},{10,2},{12,4},{14,6},{1,9},{3,11}... | collective-permute-start | bytes 294920 | tf_op jit(solution)/shard_map/ppermute | solution.py:574
  32.9 0.0 collective-permute-done.5.outer
  32.9 0.0 collective-permute-done.6.inner
  32.9 14.3 %near_remote.1 = (f32[32,4096]{1,0:T(8,128)S(1)}, f32[32,2048]{1,0:T(8,128)S(1)}) custom-call(s32[32,32]{1,0:T(8,128)S(1)} %get-tuple-element.69.tab, s32[6,32]{1,0:T(8,128)S(1)} %get-tuple-element.70.far_src, s32[32]{0:T(128)S(1)} %get-tuple-element.71.far_count, bf16[64,4096]{1,0:T(8,128)(2,1)S(1)} %collective-permute-done.5.outer, ...), custom_call_target="tpu_custom_call" | custom-call | flops 14000000 | bytes 42000000 | tf_op jit(solution)/shard_map/near_remote/pallas_call | solution.py:621
  47.2 0.0 collective-permute-done.4.theirs
  47.2 2.7 %downward.1 = f32[32,4096]{1,0:T(8,128)} custom-call(s32[6,14]{1,0:T(8,128)S(1)} %get-tuple-element.40.top_src, s32[14]{0:T(128)S(1)} %get-tuple-element.41.top_count, f32[192,128]{1,0:T(8,128)S(1)} %constant_dynamic-update-slice_fusion.mine, f32[192,128]{1,0:T(8,128)S(1)} %collective-permute-done.4.theirs, f32[3,64,384]{2,1,0:T(8,128)S(1)} %top_kernels.1.tops, ...), custom_call_target="tpu_custom_call" | custom-call | flops 4000000 | bytes 12000000 | tf_op jit(solution)/shard_map/downward/pallas_call | solution.py:636
  (5 shorter events, 0.0 us)
Async XLA Ops:
  0.0 3.0 %collective-permute-start = (bf16[32,4096]{1,0:T(8,128)(2,1)}, bf16[32,4096]{1,0:T(8,128)(2,1)S(1)}, u32[]{:S(2)}, u32[]{:S(2)}) collective-permute-start(bf16[32,4096]{1,0:T(8,128)(2,1)} %refs_0_.1), channel_id=1, source_target_pairs={{0,1},{1,0},{2,3},{3,2},{4,5},{5,4},{6,7},{7,6},{8,9},{9,8},{10,11... | collective-permute-start | bytes 786440 | tf_op jit(solution)/shard_map/ppermute | solution.py:514
  8.6 3.1 %collective-permute-start.1 = (f32[48,128]{1,0:T(8,128)S(1)}, f32[48,128]{1,0:T(8,128)S(1)}, u32[]{:S(2)}, u32[]{:S(2)}) collective-permute-start(f32[48,128]{1,0:T(8,128)S(1)} %get-tuple-element.49), channel_id=1, source_target_pairs={{0,1},{1,0},{2,3},{3,2},{4,5},{5,4},{6,7},{7,6},{8,9},{9,8},{10,11... | collective-permute-start | bytes 73736 | tf_op jit(solution)/shard_map/ppermute | solution.py:576
  11.7 6.4 %collective-permute-start.2 = (f32[48,128]{1,0:T(8,128)S(1)}, f32[48,128]{1,0:T(8,128)S(1)}, u32[]{:S(2)}, u32[]{:S(2)}) collective-permute-start(f32[48,128]{1,0:T(8,128)S(1)} %add.3), channel_id=1, source_target_pairs={{0,2},{2,0},{4,6},{6,4},{8,10},{10,8},{12,14},{14,12},{1,3},{3,1},... | collective-permute-start | bytes 73736 | tf_op jit(solution)/shard_map/ppermute | solution.py:574
  13.3 19.5 %collective-permute-start.5 = (bf16[64,4096]{1,0:T(8,128)(2,1)S(1)}, bf16[64,4096]{1,0:T(8,128)(2,1)S(1)}, u32[]{:S(2)}, u32[]{:S(2)}) collective-permute-start(bf16[64,4096]{1,0:T(8,128)(2,1)S(1)} %get-tuple-element.65.pack), channel_id=1, source_target_pairs={{1,2},{3,4},{5,6},{7,8},{9,10},{11,12},{13,14},{2,1},{4,3},{6,5},{... | collective-permute-start | bytes 1572872 | tf_op jit(solution)/shard_map/ppermute | solution.py:593
  18.2 14.7 %collective-permute-start.6 = (bf16[64,4096]{1,0:T(8,128)(2,1)S(1)}, bf16[64,4096]{1,0:T(8,128)(2,1)S(1)}, u32[]{:S(2)}, u32[]{:S(2)}) collective-permute-start(bf16[64,4096]{1,0:T(8,128)(2,1)S(1)} %get-tuple-element.65.pack), channel_id=1, source_target_pairs={{0,1},{1,0},{2,3},{3,2},{4,5},{5,4},{6,7},{7,6},{8,9},{9,8},{10,11... | collective-permute-start | bytes 1572872 | tf_op jit(solution)/shard_map/ppermute | solution.py:595
  18.3 10.4 %collective-permute-start.3 = (f32[96,128]{1,0:T(8,128)S(1)}, f32[96,128]{1,0:T(8,128)S(1)}, u32[]{:S(2)}, u32[]{:S(2)}) collective-permute-start(f32[96,128]{1,0:T(8,128)S(1)} %pad_maximum_fusion), channel_id=1, source_target_pairs={{0,4},{2,6},{4,0},{6,2},{8,12},{10,14},{12,8},{14,10},{1,5},{3,7},... | collective-permute-start | bytes 147464 | tf_op jit(solution)/shard_map/ppermute | solution.py:574
  28.6 18.5 %collective-permute-start.4 = (f32[192,128]{1,0:T(8,128)S(1)}, f32[192,128]{1,0:T(8,128)S(1)}, u32[]{:S(2)}, u32[]{:S(2)}) collective-permute-start(f32[192,128]{1,0:T(8,128)S(1)} %constant_dynamic-update-slice_fusion.mine), channel_id=1, source_target_pairs={{0,8},{2,10},{4,12},{6,14},{8,0},{10,2},{12,4},{14,6},{1,9},{3,11}... | collective-permute-start | bytes 294920 | tf_op jit(solution)/shard_map/ppermute | solution.py:574

commit v3 on v2

--- a/solution.py
+++ b/solution.py
@@ -198,19 +198,20 @@
     places[...] = jnp.zeros_like(places)
     offset = 0
     for level in range(3):
+        nodes = lax.axis_size("br") >> level
         row = offset + (lax.axis_index("br") >> level)
         places[0:3, 0:rank] = node_places(skeleton, row, rank)
         own = places[...].T
         kernels = []
         for j in range(fan):
-            there = node_places(skeleton, offset + top_src[j, row], rank)
+            there = node_places(skeleton, offset + jnp.minimum(top_src[j, row], nodes - 1), rank)
             squared = None
             for d in range(3):
                 gap = (there[d : d + 1, :] - own[0:rank, d : d + 1]) * scale
                 squared = gap * gap if squared is None else squared + gap * gap
             kernels.append(profile_of(squared))
         tops[level] = jnp.concatenate(kernels, axis=1)
-        offset += lax.axis_size("br") >> level
+        offset += nodes
 
 
 def table_height(leaves, near):
@@ -446,7 +447,7 @@
         row = offset + node
         coefs = []
         for j in range(fan):
-            source = top_src[j, row]
+            source = jnp.minimum(top_src[j, row], (branches >> level) - 1)
             coefs.append(jnp.where(j < top_count[row], coefficients(level, source), 0.0))
         fields.append(
             lax.dot_general(

time: 50.4 us -> 50.4 us (level)
  the two profiles are of different devices: /device:TPU:15 before, /device:TPU:11 now
where the time goes in v3:
time: 50.4 us; the launch traced here: 51.2 us
  Pallas kernels  38.8 us (77%)
  starting transfers between devices  12.2 us (24%)
    pallas_call x1, Pallas kernels, shards(): pl.pallas_call(near_remote, out_shape=(shape((rhs, width), f32), shape((r...  13.7 us
    pallas_call x1, Pallas kernels, local(): pl.pallas_call(near_local, out_shape=shape((rhs, width), f32), in_specs=[...  10.1 us
    ppermute x3, starting transfers between devices, shards(): lax.ppermute(x, 'br', [(i, i ^ 1 << bit) for i in range(branches)])  6.62 us
    pallas_call x1, Pallas kernels, shards(): pl.pallas_call(upward, out_shape=(shape((rhs + FEAT + rhs // 2, width), b...  5.64 us
    ppermute x1, starting transfers between devices, shards(): lax.ppermute(held, ('br', 'sub'), between + [(b, a) for a, b in between])  4.8 us
    pallas_call x1, Pallas kernels, shards(): pl.pallas_call(turn, out_shape=(shape((height, WIDE), jnp.int32),) * 2 +...  3.1 us
    pallas_call x1, Pallas kernels, shards(): pl.pallas_call(downward, out_shape=shape((rhs, width), f32), in_specs=[SM...  2.73 us
    pallas_call x1, Pallas kernels, shards(): pl.pallas_call(prepare, out_shape=tuple((like(x) for i, x in enumerate(fe...  2.27 us
  transfers between devices with their start and end apart: 7, of which 0 were waited for; matrix products, arithmetic and copies ran while one was open for 0% of the time, Pallas kernels for 60%

profile of v3, /device:TPU:11, one launch (start us, length us, event | category | flops | bytes accessed | tf_op | source)
XLA Modules:
  0.0 51.2 jit_solution(4262635554675902890)
XLA Ops:
  0.0 0.7 %collective-permute-start = (bf16[32,4096]{1,0:T(8,128)(2,1)}, bf16[32,4096]{1,0:T(8,128)(2,1)S(1)}, u32[]{:S(2)}, u32[]{:S(2)}) collective-permute-start(bf16[32,4096]{1,0:T(8,128)(2,1)} %refs_0_.1), channel_id=1, source_target_pairs={{0,1},{1,0},{2,3},{3,2},{4,5},{5,4},{6,7},{7,6},{8,9},{9,8},{10,11... | collective-permute-start | bytes 786440 | tf_op jit(solution)/shard_map/ppermute | solution.py:515
  0.7 2.3 %prepare.1 = (bf16[32,4096]{1,0:T(8,128)(2,1)S(1)}, s32[32,128]{1,0:T(8,128)S(1)}, s32[32,27]{1,0:T(8,128)S(1)}, s32[1,32]{1,0:T(1,128)S(1)}, bf16[32,64,128]{2,...) custom-call(bf16[32,4096]{1,0:T(8,128)(2,1)} %refs_0_.1, ...), custom_call_target="tpu_custom_call" | custom-call | flops 2000000 | bytes 6000000 | tf_op jit(solution)/shard_map/prepare/pallas_call | solution.py:526
  3.0 0.0 collective-permute-done.partner
  3.0 5.6 %upward.1 = (bf16[64,4096]{1,0:T(8,128)(2,1)S(1)}, f32[48,128]{1,0:T(8,128)S(1)}) custom-call(bf16[32,4096]{1,0:T(8,128)(2,1)S(1)} %get-tuple-element.42.charges, bf16[32,4096]{1,0:T(8,128)(2,1)S(1)} %collective-permute-done.partner, s32[32,128]{1,0:T(8,128)S(1)} %get-tuple-element.43.order, bf16[16,4096]{1,0:T(8,128)(2,1)S(1)} %get-tuple-element.44.feats, ...), custom_call_target="tpu_custom_call" | custom-call | flops 6000000 | bytes 18000000 | tf_op jit(solution)/shard_map/upward/pallas_call | solution.py:543
  8.6 0.0 collective-permute-start.1
  8.6 3.1 %turn.1 = (s32[32,32]{1,0:T(8,128)S(1)}, s32[32,32]{1,0:T(8,128)S(1)}, bf16[4096,48]{1,0:T(8,128)(2,1)S(1)}) custom-call(s32[32,27]{1,0:T(8,128)S(1)} %get-tuple-element.50.near_src, s32[1,32]{1,0:T(1,128)S(1)} %get-tuple-element.51.near_count, bf16[48,4096]{1,0:T(8,128)(2,1)S(1)} %get-tuple-element.52.tall), custom_call_target="tpu_custom_call" | custom-call | flops 2000000 | bytes 6000000 | tf_op jit(solution)/shard_map/turn/pallas_call | solution.py:565
  11.7 0.0 collective-permute-done.1
  11.7 0.3 collective-permute-start.2
  12.0 1.3 %top_kernels.1.tops = f32[3,64,384]{2,1,0:T(8,128)S(1)} custom-call(s32[6,14]{1,0:T(8,128)S(1)} %get-tuple-element.40.top_src, f32[3,896]{1,0:T(4,128)S(1)} %get-tuple-element.60.skeleton), custom_call_target="tpu_custom_call" | custom-call | flops 1000000 | bytes 3000000 | tf_op jit(solution)/shard_map/top_kernels/pallas_call | solution.py:582
  13.3 4.8 %collective-permute-start.5 = (bf16[64,4096]{1,0:T(8,128)(2,1)S(1)}, bf16[64,4096]{1,0:T(8,128)(2,1)S(1)}, u32[]{:S(2)}, u32[]{:S(2)}) collective-permute-start(bf16[64,4096]{1,0:T(8,128)(2,1)S(1)} %get-tuple-element.65.pack), channel_id=1, source_target_pairs={{1,2},{3,4},{5,6},{7,8},{9,10},{11,12},{13,14},{2,1},{4,3},{6,5},{... | collective-permute-start | bytes 1572872 | tf_op jit(solution)/shard_map/ppermute | solution.py:594
  18.1 0.0 collective-permute-done.2
  18.1 0.1 collective-permute-start.6
  18.2 0.3 collective-permute-start.3
  18.5 10.1 %near_local.1.start = f32[32,4096]{1,0:T(8,128)S(1)} custom-call(s32[32,32]{1,0:T(8,128)S(1)} %get-tuple-element.64.tab, bf16[64,4096]{1,0:T(8,128)(2,1)S(1)} %get-tuple-element.65.pack, bf16[4096,48]{1,0:T(8,128)(2,1)S(1)} %get-tuple-element.66.target), custom_call_target="tpu_custom_call" | custom-call | flops 6000000 | bytes 18000000 | tf_op jit(solution)/shard_map/near_local/pallas_call | solution.py:602
  28.6 0.0 collective-permute-done.3
  28.7 6.1 %collective-permute-start.4 = (f32[192,128]{1,0:T(8,128)S(1)}, f32[192,128]{1,0:T(8,128)S(1)}, u32[]{:S(2)}, u32[]{:S(2)}) collective-permute-start(f32[192,128]{1,0:T(8,128)S(1)} %constant_dynamic-update-slice_fusion.mine), channel_id=1, source_target_pairs={{0,8},{2,10},{4,12},{6,14},{8,0},{10,2},{12,4},{14,6},{1,9},{3,11}... | collective-permute-start | bytes 294920 | tf_op jit(solution)/shard_map/ppermute | solution.py:575
  34.7 0.0 collective-permute-done.5.outer
  34.7 0.0 collective-permute-done.6.inner
  34.7 13.7 %near_remote.1 = (f32[32,4096]{1,0:T(8,128)S(1)}, f32[32,2048]{1,0:T(8,128)S(1)}) custom-call(s32[32,32]{1,0:T(8,128)S(1)} %get-tuple-element.69.tab, s32[6,32]{1,0:T(8,128)S(1)} %get-tuple-element.70.far_src, s32[32]{0:T(128)S(1)} %get-tuple-element.71.far_count, bf16[64,4096]{1,0:T(8,128)(2,1)S(1)} %collective-permute-done.5.outer, ...), custom_call_target="tpu_custom_call" | custom-call | flops 14000000 | bytes 42000000 | tf_op jit(solution)/shard_map/near_remote/pallas_call | solution.py:622
  48.4 0.0 collective-permute-done.4.theirs
  48.4 2.7 %downward.1 = f32[32,4096]{1,0:T(8,128)} custom-call(s32[6,14]{1,0:T(8,128)S(1)} %get-tuple-element.40.top_src, s32[14]{0:T(128)S(1)} %get-tuple-element.41.top_count, f32[192,128]{1,0:T(8,128)S(1)} %constant_dynamic-update-slice_fusion.mine, f32[192,128]{1,0:T(8,128)S(1)} %collective-permute-done.4.theirs, f32[3,64,384]{2,1,0:T(8,128)S(1)} %top_kernels.1.tops, ...), custom_call_target="tpu_custom_call" | custom-call | flops 4000000 | bytes 12000000 | tf_op jit(solution)/shard_map/downward/pallas_call | solution.py:637
  (5 shorter events, 0.0 us)
Async XLA Ops:
  0.0 3.0 %collective-permute-start = (bf16[32,4096]{1,0:T(8,128)(2,1)}, bf16[32,4096]{1,0:T(8,128)(2,1)S(1)}, u32[]{:S(2)}, u32[]{:S(2)}) collective-permute-start(bf16[32,4096]{1,0:T(8,128)(2,1)} %refs_0_.1), channel_id=1, source_target_pairs={{0,1},{1,0},{2,3},{3,2},{4,5},{5,4},{6,7},{7,6},{8,9},{9,8},{10,11... | collective-permute-start | bytes 786440 | tf_op jit(solution)/shard_map/ppermute | solution.py:515
  8.6 3.1 %collective-permute-start.1 = (f32[48,128]{1,0:T(8,128)S(1)}, f32[48,128]{1,0:T(8,128)S(1)}, u32[]{:S(2)}, u32[]{:S(2)}) collective-permute-start(f32[48,128]{1,0:T(8,128)S(1)} %get-tuple-element.49), channel_id=1, source_target_pairs={{0,1},{1,0},{2,3},{3,2},{4,5},{5,4},{6,7},{7,6},{8,9},{9,8},{10,11... | collective-permute-start | bytes 73736 | tf_op jit(solution)/shard_map/ppermute | solution.py:577
  11.7 6.4 %collective-permute-start.2 = (f32[48,128]{1,0:T(8,128)S(1)}, f32[48,128]{1,0:T(8,128)S(1)}, u32[]{:S(2)}, u32[]{:S(2)}) collective-permute-start(f32[48,128]{1,0:T(8,128)S(1)} %add.3), channel_id=1, source_target_pairs={{0,2},{2,0},{4,6},{6,4},{8,10},{10,8},{12,14},{14,12},{1,3},{3,1},... | collective-permute-start | bytes 73736 | tf_op jit(solution)/shard_map/ppermute | solution.py:575
  13.3 21.4 %collective-permute-start.5 = (bf16[64,4096]{1,0:T(8,128)(2,1)S(1)}, bf16[64,4096]{1,0:T(8,128)(2,1)S(1)}, u32[]{:S(2)}, u32[]{:S(2)}) collective-permute-start(bf16[64,4096]{1,0:T(8,128)(2,1)S(1)} %get-tuple-element.65.pack), channel_id=1, source_target_pairs={{1,2},{3,4},{5,6},{7,8},{9,10},{11,12},{13,14},{2,1},{4,3},{6,5},{... | collective-permute-start | bytes 1572872 | tf_op jit(solution)/shard_map/ppermute | solution.py:594
  18.1 16.6 %collective-permute-start.6 = (bf16[64,4096]{1,0:T(8,128)(2,1)S(1)}, bf16[64,4096]{1,0:T(8,128)(2,1)S(1)}, u32[]{:S(2)}, u32[]{:S(2)}) collective-permute-start(bf16[64,4096]{1,0:T(8,128)(2,1)S(1)} %get-tuple-element.65.pack), channel_id=1, source_target_pairs={{0,1},{1,0},{2,3},{3,2},{4,5},{5,4},{6,7},{7,6},{8,9},{9,8},{10,11... | collective-permute-start | bytes 1572872 | tf_op jit(solution)/shard_map/ppermute | solution.py:596
  18.2 10.4 %collective-permute-start.3 = (f32[96,128]{1,0:T(8,128)S(1)}, f32[96,128]{1,0:T(8,128)S(1)}, u32[]{:S(2)}, u32[]{:S(2)}) collective-permute-start(f32[96,128]{1,0:T(8,128)S(1)} %pad_maximum_fusion), channel_id=1, source_target_pairs={{0,4},{2,6},{4,0},{6,2},{8,12},{10,14},{12,8},{14,10},{1,5},{3,7},... | collective-permute-start | bytes 147464 | tf_op jit(solution)/shard_map/ppermute | solution.py:575
  28.7 19.8 %collective-permute-start.4 = (f32[192,128]{1,0:T(8,128)S(1)}, f32[192,128]{1,0:T(8,128)S(1)}, u32[]{:S(2)}, u32[]{:S(2)}) collective-permute-start(f32[192,128]{1,0:T(8,128)S(1)} %constant_dynamic-update-slice_fusion.mine), channel_id=1, source_target_pairs={{0,8},{2,10},{4,12},{6,14},{8,0},{10,2},{12,4},{14,6},{1,9},{3,11}... | collective-permute-start | bytes 294920 | tf_op jit(solution)/shard_map/ppermute | solution.py:575
